TPU v7x, 32 devices: a whole 2x2x4 slice. The times are simulated.
32 devices in a mesh: col: 8 (over y, x, core), seq: 4 (over z).
Axes of the slice: x: 2, y: 2, z: 4, core: 2. Of those that a mesh axis runs over, the one named last changes fastest.
Arguments:
- tokens: bfloat16 [8192, 768], P(('col', 'seq')), may hold values from -6 to 6
- table_ids: int32 [8192], P(('col', 'seq')), may hold values from 0 to 2, as said below
- w_query: bfloat16 [768, 768], P(('col', 'seq')), may hold values from -0.21875 to 0.21875
- w_key: bfloat16 [768, 768], P(('col', 'seq')), may hold values from -0.21875 to 0.21875
- w_value: bfloat16 [768, 768], P(('col', 'seq')), may hold values from -0.21875 to 0.21875
- w_out: bfloat16 [768, 768], P(('col', 'seq')), may hold values from -1.75 to 1.75
- w_up: bfloat16 [768, 3072], P(('col', 'seq')), may hold values from -0.21875 to 0.21875
- w_down: bfloat16 [3072, 768], P(('col', 'seq')), may hold values from -0.109375 to 0.109375
- b_query: bfloat16 [768], P(('col', 'seq')), may hold values from -3 to 3
- b_value: bfloat16 [768], P(('col', 'seq')), may hold values from -3 to 3
- b_out: bfloat16 [768], P(('col', 'seq')), may hold values from -3 to 3
- b_up: bfloat16 [3072], P(('col', 'seq')), may hold values from -3 to 3
- b_down: bfloat16 [768], P(('col', 'seq')), may hold values from -3 to 3
- gain_attn: bfloat16 [768], P(('col', 'seq')), may hold values from 0.099609375 to 1.8984375
- shift_attn: bfloat16 [768], P(('col', 'seq')), may hold values from -3 to 3
- gain_ffn: bfloat16 [768], P(('col', 'seq')), may hold values from 0.099609375 to 1.8984375
- shift_ffn: bfloat16 [768], P(('col', 'seq')), may hold values from -3 to 3
- cotangent: bfloat16 [8192, 768], P(('col', 'seq')), may hold values from -6 to 6
Outputs:
- layer_out: bfloat16 [8192, 768], P(('col', 'seq'))
- grad_tokens: float32 [8192, 768], P(('col', 'seq'))
- grad_w_query: float32 [768, 768], P(('col', 'seq'))
- grad_w_key: float32 [768, 768], P(('col', 'seq'))
- grad_w_value: float32 [768, 768], P(('col', 'seq'))
- grad_w_out: float32 [768, 768], P(('col', 'seq'))
- grad_w_up: float32 [768, 3072], P(('col', 'seq'))
- grad_w_down: float32 [3072, 768], P(('col', 'seq'))
- grad_b_query: float32 [768], P(('col', 'seq'))
- grad_b_value: float32 [768], P(('col', 'seq'))
- grad_b_out: float32 [768], P(('col', 'seq'))
- grad_b_up: float32 [3072], P(('col', 'seq'))
- grad_b_down: float32 [768], P(('col', 'seq'))
- grad_gain_attn: float32 [768], P(('col', 'seq'))
- grad_shift_attn: float32 [768], P(('col', 'seq'))
- grad_gain_ffn: float32 [768], P(('col', 'seq'))
- grad_shift_ffn: float32 [768], P(('col', 'seq'))
Inputs may be any that keep to these rules, and one draw needn't show every extreme that they name: `table_ids`: each seq group holds 3 whole tables, 1 of 1024 tokens and the others of 512 tokens; every table's tokens are dealt evenly over the col devices of its group, 512 / (the number of col devices) tokens of a short table and 1024 / (the number of col devices) of a long one on each, in any order within a device.
All inputs are finite; a program needn't handle non-finite values.
Results may differ from a plain program's by a relative error of at most 0.02.
Values may be sent and summed in bfloat16 or wider, within the bound.
No kernel may reach another device: no remote copies, remote signals or barrier semaphores. Data moves between devices by JAX's collectives and lax.ppermute only.
A program may use at most 192 MiB of HBM per device.

v0:
```python
import jax
import jax.numpy as jnp
from jax import lax
from jax.sharding import PartitionSpec as P

H = 12
HD = 64


NEG_BIG = -1e30
NORM_EPS = 1e-12
LOW_TYPE = jnp.bfloat16
FULL_TYPE = jnp.float32


def block_length(unit_rows):
    target = unit_rows * max(1, -(-512 // unit_rows))
    return target


def layer_norm(values, gain, shift):
    center = values - jnp.mean(values, axis=-1, keepdims=True)
    spread = jnp.mean(center * center, axis=-1, keepdims=True)
    return center * lax.rsqrt(spread + NORM_EPS) * gain + shift


def gelu_exact(values):
    return jax.nn.gelu(values, approximate=False)


def project(left, right, bias):
    return jnp.dot(left, right, preferred_element_type=FULL_TYPE) + bias.astype(FULL_TYPE)


def attend(running, query_heads, query_ids, key_slab, value_slab, key_ids):
    maxima, totals, weighted = running
    scores = (
        jnp.einsum("thd,shd->hts", query_heads, key_slab, preferred_element_type=FULL_TYPE) * 0.125
    )
    visible = (query_ids[:, None] == key_ids[None, :])[None]
    scores = jnp.where(visible, scores, NEG_BIG)
    new_max = jnp.maximum(maxima, jnp.max(scores, axis=2))
    rescale = jnp.exp(maxima - new_max)
    exponents = jnp.where(visible, jnp.exp(scores - new_max[:, :, None]), 0.0)
    totals = totals * rescale + jnp.sum(exponents, axis=2)
    weighted = weighted * rescale[:, :, None] + jnp.einsum(
        "hts,shd->htd", exponents.astype(LOW_TYPE), value_slab, preferred_element_type=FULL_TYPE
    )
    return (new_max, totals, weighted)


def grad_block(
    query_heads, dout_heads, log_totals, row_delta, query_ids, key_slab, value_slab, key_ids
):
    scores = (
        jnp.einsum("thd,shd->hts", query_heads, key_slab, preferred_element_type=FULL_TYPE) * 0.125
    )
    visible = (query_ids[:, None] == key_ids[None, :])[None]
    probabilities = jnp.where(visible, jnp.exp(scores - log_totals[:, :, None]), 0.0)
    grad_value = jnp.einsum(
        "hts,thd->shd", probabilities.astype(LOW_TYPE), dout_heads, preferred_element_type=FULL_TYPE
    )
    grad_probs = jnp.einsum(
        "thd,shd->hts", dout_heads, value_slab, preferred_element_type=FULL_TYPE
    )
    grad_scores = (probabilities * (grad_probs - row_delta[:, :, None])).astype(LOW_TYPE)
    grad_query = (
        jnp.einsum("hts,shd->thd", grad_scores, key_slab, preferred_element_type=FULL_TYPE) * 0.125
    )
    grad_key = (
        jnp.einsum("hts,thd->shd", grad_scores, query_heads, preferred_element_type=FULL_TYPE)
        * 0.125
    )
    return (grad_query, grad_key, grad_value)


def per_device(
    tokens,
    table_ids,
    w_query,
    w_key,
    w_value,
    w_out,
    w_up,
    w_down,
    b_query,
    b_value,
    b_out,
    b_up,
    b_down,
    gain_attn,
    shift_attn,
    gain_ffn,
    shift_ffn,
    cotangent,
):
    shards = (
        w_query,
        w_key,
        w_value,
        w_out,
        w_up,
        w_down,
        b_query,
        b_value,
        b_out,
        b_up,
        b_down,
        gain_attn,
        shift_attn,
        gain_ffn,
        shift_ffn,
    )
    gathered = (
        lax.all_gather(shards[0], ("col", "seq"), axis=0, tiled=True),
        lax.all_gather(shards[1], ("col", "seq"), axis=0, tiled=True),
        lax.all_gather(shards[2], ("col", "seq"), axis=0, tiled=True),
        lax.all_gather(shards[3], ("col", "seq"), axis=0, tiled=True),
        lax.all_gather(shards[4], ("col", "seq"), axis=0, tiled=True),
        lax.all_gather(shards[5], ("col", "seq"), axis=0, tiled=True),
        lax.all_gather(shards[6], ("col", "seq"), axis=0, tiled=True),
        lax.all_gather(shards[7], ("col", "seq"), axis=0, tiled=True),
        lax.all_gather(shards[8], ("col", "seq"), axis=0, tiled=True),
        lax.all_gather(shards[9], ("col", "seq"), axis=0, tiled=True),
        lax.all_gather(shards[10], ("col", "seq"), axis=0, tiled=True),
        lax.all_gather(shards[11], ("col", "seq"), axis=0, tiled=True),
        lax.all_gather(shards[12], ("col", "seq"), axis=0, tiled=True),
        lax.all_gather(shards[13], ("col", "seq"), axis=0, tiled=True),
        lax.all_gather(shards[14], ("col", "seq"), axis=0, tiled=True),
    )
    query_mat, key_mat, value_mat, out_mat, up_mat, down_mat = (
        gathered[0],
        gathered[1],
        gathered[2],
        gathered[3],
        gathered[4],
        gathered[5],
    )
    query_bias, value_bias, out_bias, up_bias, down_bias = (
        gathered[6],
        gathered[7],
        gathered[8],
        gathered[9],
        gathered[10],
    )
    attn_gain, attn_shift, ffn_gain, ffn_shift = (
        gathered[11],
        gathered[12],
        gathered[13],
        gathered[14],
    )
    tok_rows = tokens.shape[0]
    ids_all = lax.all_gather(table_ids, "col", axis=0, tiled=True)
    inputs = tokens.astype(FULL_TYPE)
    queries = project(tokens, query_mat, query_bias).astype(LOW_TYPE)
    keys = jnp.dot(tokens, key_mat, preferred_element_type=FULL_TYPE).astype(LOW_TYPE)
    values = project(tokens, value_mat, value_bias).astype(LOW_TYPE)
    query_heads = queries.reshape(tok_rows, H, HD)
    starting = (
        jnp.full((H, tok_rows), NEG_BIG, FULL_TYPE),
        jnp.zeros((H, tok_rows), FULL_TYPE),
        jnp.zeros((H, tok_rows, HD), FULL_TYPE),
    )
    running = starting
    key_rows = lax.all_gather(keys, "col", axis=0, tiled=True)
    value_rows = lax.all_gather(values, "col", axis=0, tiled=True)
    row_count = key_rows.shape[0]
    length = block_length(tok_rows)
    blocks = row_count // length

    def advance(current, pieces):
        return (attend(current, query_heads, table_ids, pieces[0], pieces[1], pieces[2]), None)

    running, _ = lax.scan(
        advance,
        running,
        (
            key_rows.reshape(blocks, length, H, HD),
            value_rows.reshape(blocks, length, H, HD),
            ids_all.reshape(blocks, length),
        ),
    )
    maxima, totals, weighted = running
    attn_heads = weighted / totals[:, :, None]
    log_totals = maxima + jnp.log(totals)
    attn_low = attn_heads.transpose(1, 0, 2).reshape(tok_rows, H * HD).astype(LOW_TYPE)
    hidden = inputs + project(attn_low, out_mat, out_bias)
    normed, norm_first = jax.vjp(
        layer_norm, hidden, attn_gain.astype(FULL_TYPE), attn_shift.astype(FULL_TYPE)
    )
    normed_low = normed.astype(LOW_TYPE)
    upper = project(normed_low, up_mat, up_bias)
    active, gelu_back = jax.vjp(gelu_exact, upper)
    active_low = active.astype(LOW_TYPE)
    summed = normed + project(active_low, down_mat, down_bias)
    result, norm_second = jax.vjp(
        layer_norm, summed, ffn_gain.astype(FULL_TYPE), ffn_shift.astype(FULL_TYPE)
    )
    again = (
        lax.all_gather(w_query, ("col", "seq"), axis=0, tiled=True),
        lax.all_gather(w_key, ("col", "seq"), axis=0, tiled=True),
        lax.all_gather(w_value, ("col", "seq"), axis=0, tiled=True),
        lax.all_gather(w_out, ("col", "seq"), axis=0, tiled=True),
        lax.all_gather(w_up, ("col", "seq"), axis=0, tiled=True),
        lax.all_gather(w_down, ("col", "seq"), axis=0, tiled=True),
    )
    query_mat, key_mat, value_mat, out_mat, up_mat, down_mat = (
        again[0],
        again[1],
        again[2],
        again[3],
        again[4],
        again[5],
    )
    d_summed, d_ffn_gain, d_ffn_shift = norm_second(cotangent.astype(FULL_TYPE))
    d_down = d_summed.astype(LOW_TYPE)
    grad_down = jnp.einsum("tf,td->fd", active_low, d_down, preferred_element_type=FULL_TYPE)
    d_active = jnp.einsum("td,fd->tf", d_down, down_mat, preferred_element_type=FULL_TYPE)
    d_upper = gelu_back(d_active)[0].astype(LOW_TYPE)
    grad_up = jnp.einsum("td,tf->df", normed_low, d_upper, preferred_element_type=FULL_TYPE)
    d_normed = d_summed + jnp.einsum("tf,df->td", d_upper, up_mat, preferred_element_type=FULL_TYPE)
    d_hidden, d_attn_gain, d_attn_shift = norm_first(d_normed)
    d_branch = d_hidden.astype(LOW_TYPE)
    grad_out = jnp.einsum("tc,td->cd", attn_low, d_branch, preferred_element_type=FULL_TYPE)
    d_attn = jnp.einsum("td,cd->tc", d_branch, out_mat, preferred_element_type=FULL_TYPE).astype(
        LOW_TYPE
    )
    dout_heads = d_attn.reshape(tok_rows, H, HD)
    row_delta = jnp.einsum("thd,htd->ht", dout_heads.astype(FULL_TYPE), attn_heads)
    key_all, value_all = (
        lax.all_gather(keys, "col", axis=0, tiled=True),
        lax.all_gather(values, "col", axis=0, tiled=True),
    )
    total_rows = key_all.shape[0]
    length = block_length(tok_rows)
    blocks = total_rows // length

    def key_pass(grad_sum, pieces):
        grad_query_part, grad_key_part, grad_value_part = grad_block(
            query_heads,
            dout_heads,
            log_totals,
            row_delta,
            table_ids,
            pieces[0],
            pieces[1],
            pieces[2],
        )
        return (grad_sum + grad_query_part, (grad_key_part, grad_value_part))

    query_sum, (key_parts, value_parts) = lax.scan(
        key_pass,
        jnp.zeros((tok_rows, H, HD), FULL_TYPE),
        (
            key_all.reshape(blocks, length, H, HD),
            value_all.reshape(blocks, length, H, HD),
            ids_all.reshape(blocks, length),
        ),
    )
    key_sum, value_sum = (
        lax.psum_scatter(
            key_parts.reshape(total_rows, H * HD).astype(jnp.bfloat16),
            "col",
            scatter_dimension=0,
            tiled=True,
        ).astype(jnp.float32),
        lax.psum_scatter(
            value_parts.reshape(total_rows, H * HD).astype(jnp.bfloat16),
            "col",
            scatter_dimension=0,
            tiled=True,
        ).astype(jnp.float32),
    )
    query_sum = query_sum.reshape(tok_rows, H * HD)
    query_low = query_sum.astype(LOW_TYPE)
    key_low = key_sum.astype(LOW_TYPE)
    value_low = value_sum.astype(LOW_TYPE)
    grad_query = jnp.einsum("tc,td->cd", tokens, query_low, preferred_element_type=FULL_TYPE)
    grad_key = jnp.einsum("tc,td->cd", tokens, key_low, preferred_element_type=FULL_TYPE)
    grad_value = jnp.einsum("tc,td->cd", tokens, value_low, preferred_element_type=FULL_TYPE)
    d_tokens = d_hidden + jnp.einsum(
        "td,cd->tc", query_low, query_mat, preferred_element_type=FULL_TYPE
    )
    d_tokens = d_tokens + jnp.einsum(
        "td,cd->tc", key_low, key_mat, preferred_element_type=FULL_TYPE
    )
    d_tokens = d_tokens + jnp.einsum(
        "td,cd->tc", value_low, value_mat, preferred_element_type=FULL_TYPE
    )
    sums_local = (
        grad_query,
        grad_key,
        grad_value,
        grad_out,
        grad_up,
        grad_down,
        jnp.sum(query_low.astype(FULL_TYPE), axis=0),
        jnp.sum(value_low.astype(FULL_TYPE), axis=0),
        jnp.sum(d_branch.astype(FULL_TYPE), axis=0),
        jnp.sum(d_upper.astype(FULL_TYPE), axis=0),
        jnp.sum(d_down.astype(FULL_TYPE), axis=0),
        d_attn_gain,
        d_attn_shift,
        d_ffn_gain,
        d_ffn_shift,
    )
    owned = (
        lax.psum_scatter(sums_local[0], ("col", "seq"), scatter_dimension=0, tiled=True),
        lax.psum_scatter(sums_local[1], ("col", "seq"), scatter_dimension=0, tiled=True),
        lax.psum_scatter(sums_local[2], ("col", "seq"), scatter_dimension=0, tiled=True),
        lax.psum_scatter(sums_local[3], ("col", "seq"), scatter_dimension=0, tiled=True),
        lax.psum_scatter(sums_local[4], ("col", "seq"), scatter_dimension=0, tiled=True),
        lax.psum_scatter(sums_local[5], ("col", "seq"), scatter_dimension=0, tiled=True),
        lax.psum_scatter(sums_local[6], ("col", "seq"), scatter_dimension=0, tiled=True),
        lax.psum_scatter(sums_local[7], ("col", "seq"), scatter_dimension=0, tiled=True),
        lax.psum_scatter(sums_local[8], ("col", "seq"), scatter_dimension=0, tiled=True),
        lax.psum_scatter(sums_local[9], ("col", "seq"), scatter_dimension=0, tiled=True),
        lax.psum_scatter(sums_local[10], ("col", "seq"), scatter_dimension=0, tiled=True),
        lax.psum_scatter(sums_local[11], ("col", "seq"), scatter_dimension=0, tiled=True),
        lax.psum_scatter(sums_local[12], ("col", "seq"), scatter_dimension=0, tiled=True),
        lax.psum_scatter(sums_local[13], ("col", "seq"), scatter_dimension=0, tiled=True),
        lax.psum_scatter(sums_local[14], ("col", "seq"), scatter_dimension=0, tiled=True),
    )
    return (result.astype(LOW_TYPE), d_tokens) + tuple(owned)


def solution(mesh):
    placed = (
        P(("col", "seq"), None),
        P(("col", "seq")),
        P(("col", "seq"), None),
        P(("col", "seq"), None),
        P(("col", "seq"), None),
        P(("col", "seq"), None),
        P(("col", "seq"), None),
        P(("col", "seq"), None),
        P(("col", "seq")),
        P(("col", "seq")),
        P(("col", "seq")),
        P(("col", "seq")),
        P(("col", "seq")),
        P(("col", "seq")),
        P(("col", "seq")),
        P(("col", "seq")),
        P(("col", "seq")),
        P(("col", "seq"), None),
    )
    return jax.shard_map(
        per_device,
        mesh=mesh,
        in_specs=placed,
        out_specs=(
            P(("col", "seq"), None),
            P(("col", "seq"), None),
            P(("col", "seq"), None),
            P(("col", "seq"), None),
            P(("col", "seq"), None),
            P(("col", "seq"), None),
            P(("col", "seq"), None),
            P(("col", "seq"), None),
            P(("col", "seq")),
            P(("col", "seq")),
            P(("col", "seq")),
            P(("col", "seq")),
            P(("col", "seq")),
            P(("col", "seq")),
            P(("col", "seq")),
            P(("col", "seq")),
            P(("col", "seq")),
        ),
        check_vma=False,
    )
```

profile of v0, /device:TPU:0, one launch (start us, length us, event | category | flops | bytes accessed | tf_op | source)
XLA Modules:
  0.0 1332.2 jit_solution(17562891585911939275)
XLA Ops:
  17.0 42.4 %all-reduce.19 = (bf16[3072]{0:T(1024)(128)(2,1)S(1)}, bf16[768]{0:T(1024)(128)(2,1)S(1)}, bf16[768]{0:T(1024)(128)(2,1)S(1)}, bf16[768]{0:T(1024)(128)(2,1)S(1)...) all-reduce(bf16[3072]{0:T(1024)(128)(2,1)S(1)} %dynamic-update-slic, ...), channel_id=1, replica_groups=mesh['col'=8,'seq'=4] {'col','seq'}, use_global_device_ids=true, to_apply=%add.5 | all-reduce | flops 9216 | bytes 36864
  59.4 8.6 all-gather.16.cloned.1.call-done
  70.8 53.0 %all-gather.10.cloned.1.call-done = bf16[768,768]{1,0:T(8,128)(2,1)} async-done(((bf16[24,768]{1,0:T(8,128)(2,1)}), bf16[768,768]{1,0:T(8,128)(2,1)}) %all-gather.10.cloned.1.call-update) | async-done | bytes 1179664 | tf_op jit(solution)/shard_map/all_gather | solution.py:116
  128.6 9.1 all-gather
  142.4 37.2 %all-gather.14.cloned.1.call-done = bf16[768,768]{1,0:T(8,128)(2,1)} async-done(((bf16[24,768]{1,0:T(8,128)(2,1)}), bf16[768,768]{1,0:T(8,128)(2,1)}) %all-gather.14.cloned.1.call-update) | async-done | bytes 1179664 | tf_op jit(solution)/shard_map/all_gather | solution.py:115
  181.5 31.1 %all-gather.18.cloned.1.call-done = bf16[2048,768]{1,0:T(8,128)(2,1)} async-done(((bf16[256,768]{1,0:T(8,128)(2,1)}), bf16[2048,768]{1,0:T(8,128)(2,1)}) %all-gather.18.cloned.1.call-update) | async-done | bytes 3145744 | tf_op jit(solution)/shard_map/all_gather | solution.py:166
  215.8 4.0 reshape.194
  219.8 4.4 copy.74
  224.2 23.1 %all-gather.12.cloned.1.call-done = bf16[2048,768]{1,0:T(8,128)(2,1)} async-done(((bf16[256,768]{1,0:T(8,128)(2,1)}), bf16[2048,768]{1,0:T(8,128)(2,1)}) %all-gather.12.cloned.1.call-update) | async-done | bytes 3145744 | tf_op jit(solution)/shard_map/all_gather | solution.py:165
  250.5 4.0 reshape.192
  257.1 61.2 %while.30 = (s32[]{:T(128)}, f32[12,256]{1,0:T(8,128)S(1)}, f32[12,256]{1,0:T(8,128)}, f32[12,256,64]{1,2,0:T(8,128)}, s32[256]{0:T(256)}, /*index=5*/s32[4,512]...) while((s32[]{:T(128)}, f32[12,256]{1,0:T(8,128)S(1)}, ...), condition=%wide.region_3.4_spmd.clone, body=%wide.region_0.3_spmd.clone.sunk | while | flops 423836672 | bytes 49454860 | solution.py:174
  258.7 4.4 fusion.137
  263.8 4.4 fusion.138
  273.7 4.4 fusion.137
  278.9 4.4 fusion.138
  283.5 4.0 fusion.140
  289.1 4.4 fusion.137
  294.2 4.4 fusion.138
  298.9 4.0 fusion.140
  304.4 4.4 fusion.137
  309.6 4.4 fusion.138
  314.3 4.0 fusion.140
  324.7 44.7 %all-gather.22.cloned.1.call-done = bf16[768,3072]{1,0:T(8,128)(2,1)} async-done(((bf16[24,3072]{1,0:T(8,128)(2,1)}), bf16[768,3072]{1,0:T(8,128)(2,1)}) %all-gather.22.cloned.1.call-update) | async-done | bytes 4718608 | tf_op jit(solution)/shard_map/all_gather | solution.py:119
  369.4 12.1 multiply_convert_fusion
  381.5 53.1 %all-gather.24.cloned.1.call-done = bf16[3072,768]{1,0:T(8,128)(2,1)} async-done(((bf16[96,768]{1,0:T(8,128)(2,1)}), bf16[3072,768]{1,0:T(8,128)(2,1)}) %all-gather.24.cloned.1.call-update) | async-done | bytes 4718608 | tf_op jit(solution)/shard_map/all_gather | solution.py:120
  434.7 4.6 fusion.70
  455.7 66.5 %while.31 = (s32[]{:T(128)}, f32[256,12,64]{0,2,1:T(8,128)}, bf16[4,512,12,64]{1,3,2,0:T(8,128)(2,1)}, bf16[4,512,12,64]{1,3,2,0:T(8,128)(2,1)}, bf16[4,512,12,6...) while((s32[]{:T(128)}, f32[256,12,64]{0,2,1:T(8,128)}, ...), condition=%wide.region_13.14_spmd.clone, body=%wide.region_12.13_spmd.clone.sunk | while | flops 1023475712 | bytes 92079568 | solution.py:251
  458.7 3.8 fusion.152
  467.2 5.2 bitcast_dynamic-update-slice_fusion.5
  475.0 3.8 fusion.152
  483.8 5.2 bitcast_dynamic-update-slice_fusion.5
  491.6 3.8 fusion.152
  500.3 5.2 bitcast_dynamic-update-slice_fusion.5
  508.1 3.8 fusion.152
  516.9 5.2 bitcast_dynamic-update-slice_fusion.5
  522.1 4.3 copy.78
  529.4 4.3 copy.79
  543.0 31.3 %reduce-scatter.15.cloned.1.call-done = bf16[256,768]{0,1:T(8,128)(2,1)} async-done(((bf16[2048,768]{0,1:T(8,128)(2,1)}), bf16[256,768]{0,1:T(8,128)(2,1)}) %reduce-scatter.15.cloned.1.call-update) | async-done | bytes 393232 | tf_op jit(solution)/shard_map/reduce_scatter | solution.py:261
  578.0 46.3 %reduce-scatter.17.cloned.1.call-done = bf16[256,768]{0,1:T(8,128)(2,1)} async-done(((bf16[2048,768]{0,1:T(8,128)(2,1)}), bf16[256,768]{0,1:T(8,128)(2,1)}) %reduce-scatter.17.cloned.1.call-update) | async-done | bytes 393232 | tf_op jit(solution)/shard_map/reduce_scatter | solution.py:267
  629.1 5.9 fusion.63
  636.5 5.1 fusion.72
  644.8 40.5 %all-reduce.18 = (f32[768]{0:T(1024)S(1)}, f32[768]{0:T(1024)S(1)}, f32[768]{0:T(1024)S(1)}, f32[3072]{0:T(1024)S(1)}, f32[768]{0:T(1024)S(1)}, /*index=5*/f32[7...) all-reduce(f32[768]{0:T(1024)S(1)} %copy-done.54, ...), channel_id=10, replica_groups=mesh['col'=8,'seq'=4] {'col','seq'}, use_global_device_ids=true, to_apply=%region_23.24.clone | all-reduce | flops 9216 | bytes 73728
  693.5 36.1 %reduce-scatter.19.cloned.1.call-done = f32[24,768]{1,0:T(8,128)} async-done(((f32[768,768]{1,0:T(8,128)}), f32[24,768]{1,0:T(8,128)}) %reduce-scatter.19.cloned.1.call-update) | async-done | bytes 73744 | tf_op jit(solution)/shard_map/reduce_scatter | solution.py:311
  729.6 104.6 %reduce-scatter.25.cloned.1.call-done = f32[24,768]{1,0:T(8,128)} async-done(((f32[768,768]{1,0:T(8,128)}), f32[24,768]{1,0:T(8,128)}) %reduce-scatter.25.cloned.1.call-update) | async-done | bytes 73744
  834.2 103.9 %reduce-scatter.27.cloned.1.call-done = f32[24,768]{1,0:T(8,128)} async-done(((f32[768,768]{1,0:T(8,128)}), f32[24,768]{1,0:T(8,128)}) %reduce-scatter.27.cloned.1.call-update) | async-done | bytes 73744
  938.1 104.6 %reduce-scatter.29.cloned.1.call-done = f32[24,768]{1,0:T(8,128)} async-done(((f32[768,768]{1,0:T(8,128)}), f32[24,768]{1,0:T(8,128)}) %reduce-scatter.29.cloned.1.call-update) | async-done | bytes 73744
  1042.7 140.7 %reduce-scatter.21.cloned.1.call-done = f32[24,3072]{1,0:T(8,128)} async-done(((f32[768,3072]{1,0:T(8,128)}), f32[24,3072]{1,0:T(8,128)}) %reduce-scatter.21.cloned.1.call-update) | async-done | bytes 294928 | tf_op jit(solution)/shard_map/reduce_scatter | solution.py:312
  1183.4 142.1 %reduce-scatter.23.cloned.1.call-done = f32[96,768]{1,0:T(8,128)} async-done(((f32[3072,768]{1,0:T(8,128)}), f32[96,768]{1,0:T(8,128)}) %reduce-scatter.23.cloned.1.call-update) | async-done | bytes 294928 | tf_op jit(solution)/shard_map/reduce_scatter | solution.py:313
  (393 shorter events, 132.0 us)
Async XLA Ops:
  7.2 172.4 %copy-start.10 = (bf16[256,768]{1,0:T(8,128)(2,1)S(1)}, bf16[256,768]{1,0:T(8,128)(2,1)}, u32[]{:S(2)}) copy-start(bf16[256,768]{1,0:T(8,128)(2,1)} %param.22) | copy-start | bytes 1179652
  7.2 121.4 %copy-start.40 = (s32[256]{0:T(256)S(1)}, s32[256]{0:T(256)}, u32[]{:S(2)}) copy-start(s32[256]{0:T(256)} %param.23) | copy-start | bytes 3076
  7.2 60.8 %all-gather.16.cloned.1.call-start = ((), (), s32[]{:S(2)}) async-start(), calls=%async_computation.11 | async-start | bytes 1216512 | tf_op jit(solution)/shard_map/all_gather | solution.py:117
  7.9 115.8 %all-gather.10.cloned.1.call-start = ((), (), s32[]{:S(2)}) async-start(), calls=%async_computation.8 | async-start | bytes 1216512 | tf_op jit(solution)/shard_map/all_gather | solution.py:116
  8.7 170.9 %all-gather.14.cloned.1.call-start = ((), (), s32[]{:S(2)}) async-start(), calls=%async_computation.10 | async-start | bytes 1216512 | tf_op jit(solution)/shard_map/all_gather | solution.py:115
  9.4 203.2 %all-gather.18.cloned.1.call-start = ((), (), s32[]{:S(2)}) async-start(), calls=%async_computation.12 | async-start | bytes 3538944 | tf_op jit(solution)/shard_map/all_gather | solution.py:166
  70.7 176.6 %all-gather.12.cloned.1.call-start = ((), (), s32[]{:S(2)}) async-start(), calls=%async_computation.9 | async-start | bytes 3538944 | tf_op jit(solution)/shard_map/all_gather | solution.py:165
  126.4 193.9 %all-gather.20.cloned.1.call-start = ((), (), s32[]{:S(2)}) async-start(), calls=%async_computation.13 | async-start | bytes 1216512 | tf_op jit(solution)/shard_map/all_gather | solution.py:118
  127.0 242.5 %all-gather.22.cloned.1.call-start = ((), (), s32[]{:S(2)}) async-start(), calls=%async_computation.14 | async-start | bytes 4866048 | tf_op jit(solution)/shard_map/all_gather | solution.py:119
  127.7 306.9 %all-gather.24.cloned.1.call-start = ((), (), s32[]{:S(2)}) async-start(), calls=%async_computation.15 | async-start | bytes 4866048 | tf_op jit(solution)/shard_map/all_gather | solution.py:120
  128.5 445.9 %reduce-scatter.15.cloned.1.call-start = ((), (), s32[]{:S(2)}) async-start(), calls=%async_computation.16 | async-start | bytes 3538944 | tf_op jit(solution)/shard_map/reduce_scatter | solution.py:261
  263.8 4.7 copy-start
  263.8 4.7 copy-start.5
  278.9 4.7 copy-start
  278.9 4.7 copy-start.5
  294.2 4.5 copy-start.33
  294.2 4.7 copy-start
  294.2 4.7 copy-start.5
  309.6 4.7 copy-start
  309.6 4.7 copy-start.5
  324.7 109.9 %copy-start.37 = (f32[768]{0:T(1024)S(1)}, f32[768]{0:T(1024)}, u32[]{:S(2)}) copy-start(f32[768]{0:T(1024)} %convert_element_type.131) | copy-start | bytes 9220
  324.7 109.9 %copy-start.42 = (f32[768]{0:T(1024)S(1)}, f32[768]{0:T(1024)}, u32[]{:S(2)}) copy-start(f32[768]{0:T(1024)} %convert_element_type.132) | copy-start | bytes 9220
  324.7 109.9 %copy-start.46 = (f32[256]{0:T(256)S(1)}, f32[256]{0:T(256)}, u32[]{:S(2)}) copy-start(f32[256]{0:T(256)} %copy-done.45) | copy-start | bytes 3076
  324.7 109.9 %copy-start.55 = (f32[256]{0:T(256)S(1)}, f32[256]{0:T(256)}, u32[]{:S(2)}) copy-start(f32[256]{0:T(256)} %fusion.61) | copy-start | bytes 3076
  434.6 7.8 slice-start.2
  434.6 4.9 copy-start.27
  434.7 4.9 copy-start.44
  434.7 5.9 copy-start.49
  434.7 7.8 slice-start.3
  434.7 7.7 copy-start.61
  447.7 6.0 copy-start.36
  457.8 4.7 copy-start.1
  467.2 5.2 copy-start.3
  474.1 4.7 copy-start.1
  483.8 5.2 copy-start.3
  490.7 4.7 copy-start.1
  500.3 5.2 copy-start.3
  507.2 4.7 copy-start.1
  516.9 5.3 copy-start.3
  529.2 95.1 %reduce-scatter.17.cloned.1.call-start = ((), (), s32[]{:S(2)}) async-start(), calls=%async_computation.17 | async-start | bytes 3538944 | tf_op jit(solution)/shard_map/reduce_scatter | solution.py:267
  536.5 193.2 %reduce-scatter.19.cloned.1.call-start = ((), (), s32[]{:S(2)}) async-start(), calls=%async_computation.18 | async-start | bytes 2433024 | tf_op jit(solution)/shard_map/reduce_scatter | solution.py:311
  539.5 294.7 %reduce-scatter.25.cloned.1.call-start = ((), (), s32[]{:S(2)}) async-start(), calls=%async_computation.21 | async-start | bytes 2433024
  543.0 395.1 %reduce-scatter.27.cloned.1.call-start = ((), (), s32[]{:S(2)}) async-start(), calls=%async_computation.22 | async-start | bytes 2433024
  577.9 464.8 %reduce-scatter.29.cloned.1.call-start = ((), (), s32[]{:S(2)}) async-start(), calls=%async_computation.23 | async-start | bytes 2433024
  627.7 555.7 %reduce-scatter.21.cloned.1.call-start = ((), (), s32[]{:S(2)}) async-start(), calls=%async_computation.19 | async-start | bytes 9732096 | tf_op jit(solution)/shard_map/reduce_scatter | solution.py:312
  635.0 690.5 %reduce-scatter.23.cloned.1.call-start = ((), (), s32[]{:S(2)}) async-start(), calls=%async_computation.20 | async-start | bytes 9732096 | tf_op jit(solution)/shard_map/reduce_scatter | solution.py:313
  641.6 49.0 %copy-start.14 = (bf16[768,768]{1,0:T(8,128)(2,1)S(1)}, bf16[768,768]{1,0:T(8,128)(2,1)}, u32[]{:S(2)}) copy-start(bf16[768,768]{1,0:T(8,128)(2,1)} %all-gather.10.cloned.1.call-done) | copy-start | bytes 3538948
  685.3 6.8 copy-start.32
  (82 other events, 219.7 us)
Sparse Core Ops, SparseCore 0:
  10.8 57.1 all-gather.15
  70.8 52.8 all-gather.9
  126.5 53.0 all-gather.13
  181.3 31.2 all-gather.17
  214.9 32.3 all-gather.11
  249.9 54.0 all-gather.19
  306.9 62.5 all-gather.21
  372.2 62.3 all-gather.23
  529.3 45.0 reduce-scatter.14
  578.0 46.2 reduce-scatter.16
  630.1 99.4 reduce-scatter.18
  736.2 97.9 reduce-scatter.24
  840.1 97.9 reduce-scatter.26
  944.7 97.9 reduce-scatter.28
  1049.0 134.3 reduce-scatter.20
  1190.7 134.7 reduce-scatter.22
where the time goes:
time: 1340 us; the launch traced here: 1330 us
  waiting for transfers between devices  965 us (72%)
  matrix products  146 us (11%)
  blocking collectives  91.9 us (7%)
  local copies, waits for them, and re-layouts  74.3 us (6%)
  other arithmetic  38.6 us (3%)
  between operations  14.8 us (1%)
    unnamed x19, waiting for transfers between devices  317 us
    reduce_scatter x1, waiting for transfers between devices, per_device(): lax.psum_scatter(sums_local[5], ('col', 'seq'), scatter_dimension=0, tile...  142 us
    reduce_scatter x1, waiting for transfers between devices, per_device(): lax.psum_scatter(sums_local[4], ('col', 'seq'), scatter_dimension=0, tile...  141 us
    unnamed x2, blocking collectives  82.9 us
    all_gather x1, waiting for transfers between devices, per_device(): lax.all_gather(shards[5], ('col', 'seq'), axis=0, tiled=True)  53.1 us
    all_gather x1, waiting for transfers between devices, per_device(): lax.all_gather(shards[1], ('col', 'seq'), axis=0, tiled=True)  53 us
    reduce_scatter x1, waiting for transfers between devices, per_device(): lax.psum_scatter(value_parts.reshape(total_rows, H * HD).astype(jnp.bfloa...  46.3 us
    all_gather x1, waiting for transfers between devices, per_device(): lax.all_gather(shards[4], ('col', 'seq'), axis=0, tiled=True)  44.7 us
  transfers between devices with their start and end apart: 16, of which 15 were waited for; matrix products, arithmetic and copies ran while one was open for 12% of the time, Pallas kernels for 0%

commit v1 on v0

--- a/solution.py
+++ b/solution.py
@@ -1,6 +1,11 @@
+import functools
+
 import jax
 import jax.numpy as jnp
+import numpy as np
 from jax import lax
+from jax.experimental import pallas as pl
+from jax.experimental.pallas import tpu as pltpu
 from jax.sharding import PartitionSpec as P
 
 H = 12
@@ -324,6 +329,753 @@
     return (result.astype(LOW_TYPE), d_tokens) + tuple(owned)
 
 
+WIDTH = 768
+HALF = WIDTH // 2
+SHARD = 24
+DOWN = 96
+SLAB = (SHARD, HALF)
+VMEM_BYTES = 60 * 2**20
+F32 = jnp.float32
+BF16 = jnp.bfloat16
+
+
+def dot(left, right):
+    return jnp.dot(left, right, preferred_element_type=F32)
+
+
+def dot_nt(left, right):
+    return lax.dot_general(left, right, (((1,), (1,)), ((), ())), preferred_element_type=F32)
+
+
+def dot_tn(left, right):
+    return lax.dot_general(left, right, (((0,), (0,)), ((), ())), preferred_element_type=F32)
+
+
+def call(body, name, place, inputs, outs, scratch=(), flops=0):
+    vmem = pl.BlockSpec(memory_space=pltpu.VMEM)
+    moved = sum(a.size * a.dtype.itemsize for a in inputs)
+    moved += sum(int(np.prod(s)) * np.dtype(t).itemsize for s, t in outs)
+    return pl.pallas_call(
+        body,
+        name=name,
+        out_shape=tuple(jax.ShapeDtypeStruct(s, t) for s, t in outs),
+        in_specs=[pl.BlockSpec(memory_space=pltpu.SMEM)] + [vmem] * len(inputs),
+        out_specs=tuple(vmem for _ in outs),
+        scratch_shapes=list(scratch),
+        compiler_params=pltpu.CompilerParams(vmem_limit_bytes=VMEM_BYTES),
+        cost_estimate=pl.CostEstimate(flops=flops, bytes_accessed=moved, transcendentals=0),
+    )(place, *inputs)
+
+
+def iota(shape, dim):
+    return lax.broadcasted_iota(jnp.int32, shape, dim)
+
+
+def prep_body(place, ids, tokens, cot, wq, wk, wv, wo, wup, *rest):
+    vectors, b_up = rest[:8], rest[8]
+    perm_out, tok_out, cot_out, keep, send = rest[9:14]
+    rows8 = rest[14]
+    core, dev = place[0], place[3]
+    rows = tokens.shape[0]
+    id_j = jnp.broadcast_to(ids[...].astype(F32), (rows, rows))
+    id_i = id_j.T
+    same = jnp.where(id_i == id_j, 1.0, 0.0)
+    count_i = jnp.sum(same, axis=1, keepdims=True)
+    count_j = jnp.sum(same, axis=0, keepdims=True)
+    i, j = iota((rows, rows), 0), iota((rows, rows), 1)
+    equal = jnp.where((id_i == id_j) & (i < j), 1.0, 0.0)
+    tie = jnp.where((count_i == count_j) & (id_i < id_j), 1.0, 0.0)
+    larger = jnp.where(count_i > count_j, 1.0, 0.0)
+    position = jnp.sum(equal + tie + larger, axis=0, keepdims=True)
+    perm = jnp.where(i.astype(F32) == position, 1.0, 0.0).astype(BF16)
+    perm_out[...] = perm
+    tok_out[...] = dot(perm, tokens[...]).astype(BF16)
+    cot_out[...] = dot(perm, cot[...]).astype(BF16)
+
+    def split(mine, other):
+        for n, w in enumerate((wq, wk, wv, wo)):
+            keep[n] = w[:, mine * HALF : (mine + 1) * HALF]
+            send[n] = w[:, other * HALF : (other + 1) * HALF]
+        for u in range(4):
+            keep[4 + u] = wup[:, u * WIDTH + mine * HALF : u * WIDTH + (mine + 1) * HALF]
+            send[4 + u] = wup[:, u * WIDTH + other * HALF : u * WIDTH + (other + 1) * HALF]
+
+    @pl.when(core == 0)
+    def _():
+        split(0, 1)
+
+    @pl.when(core == 1)
+    def _():
+        split(1, 0)
+
+    for n, vector in enumerate(vectors):
+        rows8[n : n + 1, :] = vector[...].astype(F32)
+    spread = jnp.where(iota((SHARD, WIDTH), 1) == dev * SHARD + iota((SHARD, WIDTH), 0), 1.0, 0.0)
+    eight = dot(rows8[...].astype(BF16), spread.astype(BF16))
+    lane = lax.rem(dev, 8) * DOWN
+    spread_up = jnp.where(iota((DOWN, WIDTH), 1) == lane + iota((DOWN, WIDTH), 0), 1.0, 0.0)
+    one = dot(jnp.broadcast_to(b_up[...], (8, DOWN)), spread_up.astype(BF16))
+    one = jnp.where(iota((8, WIDTH), 0) == dev // 8, one, 0.0)
+    block = jnp.concatenate([eight, one, jnp.zeros((8, WIDTH), F32)], axis=0).astype(BF16)
+    for n in range(2):
+        part = block[:, n * HALF : (n + 1) * HALF]
+        keep[8 + n] = part
+        send[8 + n] = part
+
+
+def merge_body(place, keep, recv, chunk_q, chunk_u):
+    def fill(even, odd):
+        for n in range(4):
+            chunk_q[n] = even[n]
+            chunk_q[4 + n] = odd[n]
+            chunk_u[n] = even[4 + n]
+            chunk_u[4 + n] = odd[4 + n]
+
+    @pl.when(place[0] == 0)
+    def _():
+        fill(keep, recv)
+
+    @pl.when(place[0] == 1)
+    def _():
+        fill(recv, keep)
+
+    for n in (8, 9):
+        chunk_q[n] = (keep[n].astype(F32) + recv[n].astype(F32)).astype(BF16)
+
+
+def z_slot(place, k):
+    return lax.rem(place[2] + 4 - k, 4)
+
+
+def zcat_q_body(place, own, r1, r2, r3, out):
+    for k, part in enumerate((own, r1, r2, r3)):
+        slot = z_slot(place, k) * 8
+        for n in range(8):
+            out[slot + n] = part[n]
+    for n in (8, 9):
+        total = own[n].astype(F32) + r1[n].astype(F32) + r2[n].astype(F32) + r3[n].astype(F32)
+        out[24 + n] = total.astype(BF16)
+
+
+def zcat_u_body(place, own, r1, r2, r3, out):
+    for k, part in enumerate((own, r1, r2, r3)):
+        slot = z_slot(place, k) * 8
+        for n in range(8):
+            out[slot + n] = part[n]
+
+
+def pcat_d_body(place, own, r1, r2, r3, out):
+    for r, part in enumerate((own, r1, r2, r3)):
+        out[place[1] ^ r] = part[...]
+
+
+def natural(place, parts, scr, n, count=8):
+    for r, part in enumerate(parts):
+        base = (place[1] ^ r) * (8 * SHARD)
+        for z in range(4):
+            for c in range(2):
+                row = pl.multiple_of(base + c * 4 * SHARD + z * SHARD, 8)
+                scr[pl.ds(row, SHARD), :] = part[z * count + c * 4 + n].astype(F32)
+
+
+def on_core(place, action):
+    @pl.when(place[0] == 0)
+    def _():
+        action(0)
+
+    @pl.when(place[0] == 1)
+    def _():
+        action(1)
+
+
+def table_rows(tok_rows, n_col):
+    long_rows = max(2 * 512, 64 * n_col) // n_col
+    short_rows = 512 // n_col
+    units = tok_rows // short_rows
+    long_count = max(1, units // (2 * (long_rows // short_rows)))
+    tables, start = [], 0
+    for _ in range(long_count):
+        tables.append((start, long_rows))
+        start += long_rows
+    while start < tok_rows:
+        tables.append((start, short_rows))
+        start += short_rows
+    return tables
+
+
+def attend_body(tables, place, *refs):
+    toks, parts = refs[:8], refs[8:12]
+    (wqkv, wo, bias, q_out, k_out, v_out, mixed_out, mixed_low, lse_out) = refs[12:21]
+    slab, tok, q3, k3, v3 = refs[21:]
+    for n in range(3):
+        natural(place, parts, slab, n)
+        wqkv[:, n * HALF : (n + 1) * HALF] = slab[...].astype(BF16)
+    natural(place, parts, slab, 3)
+    wo[...] = slab[...].astype(BF16)
+    for n in range(2):
+        total = sum(part[32 + n].astype(F32) for part in parts)
+        bias[:, n * HALF : (n + 1) * HALF] = total
+    for n, ref in enumerate(toks):
+        tok[n] = ref[...]
+    rows = toks[0].shape[0]
+    count = len(toks)
+    k_all = dot(tok[...].reshape(count * rows, WIDTH), wqkv[:, HALF : 2 * HALF])
+    k3[...] = k_all.astype(BF16).reshape(count, rows, HALF)
+
+    def with_bias(c):
+        q_bias = bias[0:1, c * HALF : (c + 1) * HALF]
+        v_bias = bias[1:2, c * HALF : (c + 1) * HALF]
+        q_all = dot(tok[0:2].reshape(2 * rows, WIDTH), wqkv[:, :HALF]) + q_bias
+        q3[...] = q_all.astype(BF16).reshape(2, rows, HALF)
+        v_all = dot(tok[...].reshape(count * rows, WIDTH), wqkv[:, 2 * HALF :]) + v_bias
+        v3[...] = v_all.astype(BF16).reshape(count, rows, HALF)
+
+    on_core(place, with_bias)
+    q_out[...] = q3[...]
+    k_out[...] = k3[...]
+    v_out[...] = v3[...]
+    for start, size in tables:
+        lse = jnp.zeros((2 * size, 128), F32)
+        for pair in range(3):
+            lanes = slice(pair * 128, (pair + 1) * 128)
+            qp = q3[:, start : start + size, lanes].reshape(2 * size, 128)
+            kp = k3[:, start : start + size, lanes].reshape(count * size, 128)
+            vp = v3[:, start : start + size, lanes].reshape(count * size, 128)
+            low_half = iota(qp.shape, 1) < HD
+            found = []
+            for h in range(2):
+                mine = low_half if h == 0 else jnp.logical_not(low_half)
+                qm = jnp.where(mine, qp.astype(F32) * 0.125, 0.0).astype(BF16)
+                scores = dot_nt(qm, kp)
+                top = jnp.max(scores, axis=1, keepdims=True)
+                expo = jnp.exp(scores - top)
+                total = jnp.sum(expo, axis=1, keepdims=True)
+                found.append(dot(expo.astype(BF16), vp) * (1.0 / total))
+                lse = jnp.where(iota(lse.shape, 1) == pair * 2 + h, top + jnp.log(total), lse)
+            mixed = jnp.where(low_half, found[0], found[1]).reshape(2, size, 128)
+            mixed_out[:, start : start + size, lanes] = mixed
+            mixed_low[:, start : start + size, lanes] = mixed.astype(BF16)
+        lse_out[:, start : start + size, :] = lse.reshape(2, size, 128)
+
+
+def norm_stats(values):
+    center = values - jnp.mean(values, axis=1, keepdims=True)
+    spread = jnp.mean(center * center, axis=1, keepdims=True)
+    scale = lax.rsqrt(spread + NORM_EPS)
+    return center * scale, scale
+
+
+def norm_back(e, gain, vhat, scale):
+    eg = e * gain
+    mean_e = jnp.mean(eg, axis=1, keepdims=True)
+    mean_ev = jnp.mean(eg * vhat, axis=1, keepdims=True)
+    return scale * (eg - mean_e - vhat * mean_ev)
+
+
+def flip(pair):
+    return jnp.concatenate([pair[1], pair[0]], axis=0)
+
+
+def forward_body(place, tok0, tok1, mine, other, wo_mine, wo_other, bias, *refs):
+    u_parts, d_parts = refs[:4], refs[4:8]
+    (partial, vhat_out, scale_out, normed_low, active, slope, wup, wdown, mixed, wo) = refs[8:18]
+    slab, hidden = refs[18:]
+    for u in range(4):
+        natural(place, u_parts, slab, u)
+        wup[:, u * HALF : (u + 1) * HALF] = slab[...].astype(BF16)
+    for k, part in enumerate(d_parts):
+        slot = z_slot(place, k)
+        for y in range(4):
+            wdown[y * 4 + slot] = part[y]
+    rows = tok0.shape[0]
+
+    def place_halves(c):
+        mixed[:, c * HALF : (c + 1) * HALF] = mine[...].reshape(2 * rows, HALF)
+        mixed[:, (1 - c) * HALF : (2 - c) * HALF] = flip(other)
+        wo[:, c * HALF : (c + 1) * HALF] = wo_mine[...]
+        wo[:, (1 - c) * HALF : (2 - c) * HALF] = wo_other[...]
+
+    on_core(place, place_halves)
+    hidden[...] = dot(mixed[...], wo[...]) + bias[2:3, :]
+    hidden[:rows, :] += tok0[...].astype(F32)
+    hidden[rows:, :] += tok1[...].astype(F32)
+    vhat, scale = norm_stats(hidden[...])
+    vhat_out[...] = vhat
+    scale_out[...] = scale
+    normed_low[...] = (vhat * bias[4:5, :] + bias[5:6, :]).astype(BF16)
+
+    def up(c):
+        for u in range(4):
+            b = bias[8 + u : 9 + u, c * HALF : (c + 1) * HALF]
+            upper = dot(normed_low[...], wup[:, u * HALF : (u + 1) * HALF]) + b
+            cdf = 0.5 * (1.0 + lax.erf(upper * 0.7071067811865476))
+            pdf = jnp.exp(-0.5 * upper * upper) * 0.3989422804014327
+            active[:, u * HALF : (u + 1) * HALF] = (upper * cdf).astype(BF16)
+            slope[:, u * HALF : (u + 1) * HALF] = (cdf + upper * pdf).astype(BF16)
+
+    on_core(place, up)
+    partial[...] = dot(active[...], wdown[...].reshape(4 * HALF, WIDTH)).astype(BF16).reshape(2, rows, WIDTH)
+
+
+def back_ffn_body(place, perm, mine, other, vhat1, bias, cot0, cot1, slope, wup, wdown, *refs):
+    layer_out, d_summed, d_down, d_upper, d_part, sums = refs
+    rows = cot0.shape[0]
+    summed = vhat1[...] * bias[4:5, :] + bias[5:6, :] + bias[3:4, :]
+    summed = summed + mine[...].astype(F32).reshape(2 * rows, WIDTH) + flip(other).astype(F32)
+    vhat, scale = norm_stats(summed)
+    gain = bias[6:7, :]
+    result = (vhat[:rows] * gain + bias[7:8, :]).astype(BF16)
+    layer_out[...] = dot_tn(perm[...], result).astype(BF16)
+    e = jnp.concatenate([cot0[...], cot1[...]], axis=0).astype(F32)
+    sums[0:1, :] = jnp.sum(e * vhat, axis=0, keepdims=True)
+    sums[1:2, :] = jnp.sum(e, axis=0, keepdims=True)
+    grad = norm_back(e, gain, vhat, scale)
+    d_summed[...] = grad
+    low = grad.astype(BF16)
+    d_down[...] = low
+    sums[2:3, :] = jnp.sum(low.astype(F32), axis=0, keepdims=True)
+    for u in range(4):
+        d_active = dot_nt(d_down[...], wdown[u * 4 : (u + 1) * 4].reshape(HALF, WIDTH))
+        part = (d_active * slope[:, u * HALF : (u + 1) * HALF].astype(F32)).astype(BF16)
+        d_upper[:, u * HALF : (u + 1) * HALF] = part
+        half = slice((u % 2) * HALF, (u % 2 + 1) * HALF)
+        sums[3 + u // 2 : 4 + u // 2, half] = jnp.sum(part.astype(F32), axis=0, keepdims=True)
+    sums[5:8, :] = jnp.zeros((3, WIDTH), F32)
+    d_part[...] = dot_nt(d_upper[...], wup[...]).astype(BF16).reshape(2, rows, WIDTH)
+
+
+def grad_down_body(place, active, d_down, *refs):
+    outs, scr = refs[:4], refs[4]
+    scr[...] = dot_tn(active[...], d_down[...])
+    for k, out in enumerate(outs):
+        z = lax.rem(place[2] + k, 4)
+        for r in range(4):
+            row = pl.multiple_of((place[1] ^ r) * (4 * DOWN) + z * DOWN, 8)
+            out[r] = scr[pl.ds(row, DOWN), :].astype(BF16)
+
+
+def cut_slabs(place, scr, outs, n, count):
+    for r, out in enumerate(outs):
+        base = (place[1] ^ r) * (8 * SHARD)
+        for k in range(4):
+            z = lax.rem(place[2] + k, 4)
+            for c in range(2):
+                row = pl.multiple_of(base + c * 4 * SHARD + z * SHARD, 8)
+                out[k * count + c * 4 + n] = scr[pl.ds(row, SHARD), :].astype(BF16)
+
+
+def grad_up_body(place, normed_low, d_upper, *refs):
+    outs, scr = refs[:4], refs[4]
+    for u in range(4):
+        scr[...] = dot_tn(normed_low[...], d_upper[:, u * HALF : (u + 1) * HALF])
+        cut_slabs(place, scr, outs, u, 8)
+
+
+def back_attend_body(tables, place, d_summed, mine, other, vhat1, scale1, bias, wo, mixed, q3, k3, v3, lse, *refs):
+    d_hidden_out, d_branch, dq_out, dk_out, dv_out, sums, dm3 = refs
+    rows = d_hidden_out.shape[0]
+    e = d_summed[...] + mine[...].astype(F32).reshape(2 * rows, WIDTH) + flip(other).astype(F32)
+    vhat = vhat1[...]
+    sums[0:1, :] = jnp.sum(e * vhat, axis=0, keepdims=True)
+    sums[1:2, :] = jnp.sum(e, axis=0, keepdims=True)
+    d_hidden = norm_back(e, bias[4:5, :], vhat, scale1[...])
+    d_hidden_out[...] = d_hidden[:rows]
+    low = d_hidden.astype(BF16)
+    d_branch[...] = low
+    sums[2:3, :] = jnp.sum(low.astype(F32), axis=0, keepdims=True)
+    wo_rows = wo[pl.ds(pl.multiple_of(place[0] * HALF, HALF), HALF), :]
+    dm3[...] = dot_nt(d_branch[...], wo_rows).astype(BF16).reshape(2, rows, HALF)
+    count = k3.shape[0]
+    for start, size in tables:
+        for pair in range(3):
+            lanes = slice(pair * 128, (pair + 1) * 128)
+            qp = q3[:, start : start + size, lanes].reshape(2 * size, 128).astype(F32) * 0.125
+            dp = dm3[:, start : start + size, lanes].reshape(2 * size, 128).astype(F32)
+            mp = mixed[:, start : start + size, lanes].reshape(2 * size, 128)
+            kp = k3[:, start : start + size, lanes].reshape(count * size, 128)
+            vp = v3[:, start : start + size, lanes].reshape(count * size, 128)
+            logs = lse[:, start : start + size, :].reshape(2 * size, 128)
+            low_half = iota(qp.shape, 1) < HD
+            found, d_key, d_value = [], None, None
+            for h in range(2):
+                mine_h = low_half if h == 0 else jnp.logical_not(low_half)
+                qm = jnp.where(mine_h, qp, 0.0).astype(BF16)
+                dmask = jnp.where(mine_h, dp, 0.0)
+                delta = jnp.sum(dmask * mp, axis=1, keepdims=True)
+                dm = dmask.astype(BF16)
+                column = pair * 2 + h
+                probs = jnp.exp(dot_nt(qm, kp) - logs[:, column : column + 1])
+                part = dot_tn(probs.astype(BF16), dm)
+                d_value = part if d_value is None else d_value + part
+                d_scores = (probs * (dot_nt(dm, vp) - delta)).astype(BF16)
+                found.append(dot(d_scores, kp))
+                part = dot_tn(d_scores, qm)
+                d_key = part if d_key is None else d_key + part
+            d_query = jnp.where(low_half, found[0], found[1]) * 0.125
+            dq_out[:, start : start + size, lanes] = d_query.astype(BF16).reshape(2, size, 128)
+            dk_out[:, start : start + size, lanes] = d_key.astype(BF16).reshape(count, size, 128)
+            dv_out[:, start : start + size, lanes] = d_value.astype(BF16).reshape(count, size, 128)
+    sums[3:8, :] = jnp.zeros((5, WIDTH), F32)
+    q_sum = jnp.sum(dq_out[...].reshape(2 * rows, HALF).astype(F32), axis=0, keepdims=True)
+    v_sum = jnp.sum(dv_out[...].reshape(count * rows, HALF).astype(F32), axis=0, keepdims=True)
+
+    def sides(c):
+        sums[3:4, c * HALF : (c + 1) * HALF] = q_sum
+        sums[4:5, c * HALF : (c + 1) * HALF] = v_sum
+
+    on_core(place, sides)
+
+
+def grad_qkvo_body(place, *refs):
+    toks = refs[:8]
+    dq, dk, dv, mixed, d_branch, sums_ffn, sums_attn = refs[8:15]
+    outs, scr, tok, block = refs[15:19], refs[19], refs[20], refs[21]
+    rows = toks[0].shape[0]
+    count = len(toks)
+    for n, ref in enumerate(toks):
+        tok[n * rows : (n + 1) * rows, :] = ref[...]
+    scr[...] = dot_tn(tok[: 2 * rows], dq[...].reshape(2 * rows, HALF))
+    cut_slabs(place, scr, outs, 0, 8)
+    scr[...] = dot_tn(tok[...], dk[...].reshape(count * rows, HALF))
+    cut_slabs(place, scr, outs, 1, 8)
+    scr[...] = dot_tn(tok[...], dv[...].reshape(count * rows, HALF))
+    cut_slabs(place, scr, outs, 2, 8)
+
+    def out_half(c):
+        scr[...] = dot_tn(mixed[...], d_branch[:, c * HALF : (c + 1) * HALF])
+
+    on_core(place, out_half)
+    cut_slabs(place, scr, outs, 3, 8)
+    once = jnp.where(place[0] == 0, 1.0, 0.0)
+    block[...] = jnp.zeros(block.shape, F32)
+    block[0:2, :] = sums_attn[3:5, :]
+    block[2:3, :] = sums_attn[2:3, :] * once
+    block[3:4, :] = sums_ffn[2:3, :] * once
+    block[4:6, :] = sums_attn[0:2, :] * once
+    block[6:8, :] = sums_ffn[0:2, :] * once
+
+    def up_rows(c):
+        for u in range(4):
+            half = sums_ffn[3 + u // 2 : 4 + u // 2, (u % 2) * HALF : (u % 2 + 1) * HALF]
+            block[8 + u : 9 + u, c * HALF : (c + 1) * HALF] = half
+
+    on_core(place, up_rows)
+    for out in outs:
+        for n in range(2):
+            out[32 + n] = block[:, n * HALF : (n + 1) * HALF].astype(BF16)
+
+
+def grad_tok_body(place, dq, dk, dv, wqkv, same, sib):
+    rows = same.shape[1]
+    count = dk.shape[0]
+    for n in range(count):
+        total = dot_nt(dk[n], wqkv[:, HALF : 2 * HALF]) + dot_nt(dv[n], wqkv[:, 2 * HALF :])
+        if n < 2:
+            total = total + dot_nt(dq[n], wqkv[:, :HALF])
+        (same if n % 2 == 0 else sib)[n // 2] = total.astype(BF16)
+
+
+def sum_tok_body(place, same, recv, own, s1, s2, s3):
+    for r, out in enumerate((own, s1, s2, s3)):
+        out[...] = (same[r].astype(F32) + recv[r].astype(F32)).astype(BF16)
+
+
+def last_tok_body(place, perm, d_hidden, own, r1, r2, r3, out):
+    total = d_hidden[...]
+    for part in (own, r1, r2, r3):
+        total = total + part[...].astype(F32)
+    high = total.astype(BF16)
+    left = total - high.astype(F32)
+    middle = left.astype(BF16)
+    low = (left - middle.astype(F32)).astype(BF16)
+    out[...] = dot_tn(perm[...], high) + dot_tn(perm[...], middle) + dot_tn(perm[...], low)
+
+
+def added(parts, index):
+    total = parts[0][index].astype(F32)
+    for part in parts[1:]:
+        total = total + part[index].astype(F32)
+    return total
+
+
+def sum_plane_body(extra, place, own, r1, r2, r3, *outs):
+    parts = (own, r1, r2, r3)
+    for k, out in enumerate(outs):
+        for n in range(8):
+            out[n] = added(parts, k * 8 + n).astype(BF16)
+    if extra:
+        for n in range(2):
+            total = added(parts, 32 + n).astype(BF16)
+            for out in outs:
+                out[8 + n] = total
+
+
+def sum_down_body(place, own, r1, r2, r3, *outs):
+    for r, out in enumerate(outs):
+        out[...] = added((own, r1, r2, r3), r).astype(BF16)
+
+
+def last_down_body(place, own, r1, r2, r3, out):
+    out[...] = added((own, r1, r2, r3), slice(None))
+
+
+def sum_last_body(place, q0, q1, q2, q3, u0, u1, u2, u3, keep, send):
+    q_parts, u_parts = (q0, q1, q2, q3), (u0, u1, u2, u3)
+
+    def fill(mine):
+        for n in range(4):
+            keep[n] = added(q_parts, mine * 4 + n)
+            send[n] = added(q_parts, (1 - mine) * 4 + n)
+            keep[4 + n] = added(u_parts, mine * 4 + n)
+            send[4 + n] = added(u_parts, (1 - mine) * 4 + n)
+
+    on_core(place, fill)
+    for n in (8, 9):
+        total = added(q_parts, n)
+        keep[n] = total
+        send[n] = total
+
+
+def last_body(place, keep, recv, gq, gk, gv, go, gup, vectors, ups):
+    def fill(c):
+        for n, out in enumerate((gq, gk, gv, go)):
+            out[:, c * HALF : (c + 1) * HALF] = keep[n]
+            out[:, (1 - c) * HALF : (2 - c) * HALF] = recv[n]
+        for u in range(4):
+            gup[:, u * WIDTH + c * HALF : u * WIDTH + (c + 1) * HALF] = keep[4 + u]
+            gup[:, u * WIDTH + (1 - c) * HALF : u * WIDTH + (2 - c) * HALF] = recv[4 + u]
+
+    on_core(place, fill)
+    dev = place[3]
+    total = jnp.concatenate([keep[8] + recv[8], keep[9] + recv[9]], axis=1)
+    pick = jnp.where(iota((WIDTH, 128), 0) == dev * SHARD + iota((WIDTH, 128), 1), 1.0, 0.0)
+    high = lax.Precision.HIGHEST
+    vectors[...] = jnp.dot(total, pick, precision=high, preferred_element_type=F32)
+    lane = lax.rem(dev, 8) * DOWN
+    pick_up = jnp.where(iota((WIDTH, 128), 0) == lane + iota((WIDTH, 128), 1), 1.0, 0.0)
+    rows = jnp.where(iota(total.shape, 0) == 8 + dev // 8, total, 0.0)
+    row = jnp.broadcast_to(jnp.sum(rows, axis=0, keepdims=True), (8, WIDTH))
+    ups[...] = jnp.dot(row, pick_up, precision=high, preferred_element_type=F32)
+
+
+def fast_device(
+    tokens,
+    table_ids,
+    w_query,
+    w_key,
+    w_value,
+    w_out,
+    w_up,
+    w_down,
+    b_query,
+    b_value,
+    b_out,
+    b_up,
+    b_down,
+    gain_attn,
+    shift_attn,
+    gain_ffn,
+    shift_ffn,
+    cotangent,
+):
+    col, z = lax.axis_index("col"), lax.axis_index("seq")
+    place = jnp.stack([col % 2, col // 2, z, col * 4 + z]).astype(jnp.int32)
+    rows = tokens.shape[0]
+    tables = table_rows(rows, 8)
+
+    def swap(x):
+        return lax.ppermute(x, "col", [(i, i ^ 1) for i in range(8)])
+
+    def plane(x, r):
+        return lax.ppermute(x, "col", [(i, i ^ (2 * r)) for i in range(8)])
+
+    def shift(x, k):
+        return lax.ppermute(x, "seq", [(i, (i + k) % 4) for i in range(4)])
+
+    def planes(x):
+        return (x, plane(x, 1), plane(x, 2), plane(x, 3))
+
+    def shifts(x):
+        return (x, shift(x, 1), shift(x, 2), shift(x, 3))
+
+    down_parts = planes(w_down)
+    vectors = (b_query, b_value, b_out, b_down, gain_attn, shift_attn, gain_ffn, shift_ffn)
+    perm, tok_sorted, cot_sorted, keep, send = call(
+        prep_body,
+        "prep",
+        place,
+        (table_ids.reshape(1, rows), tokens, cotangent, w_query, w_key, w_value, w_out, w_up)
+        + tuple(v.reshape(1, SHARD) for v in vectors)
+        + (b_up.reshape(1, DOWN),),
+        (
+            ((rows, rows), BF16),
+            ((rows, WIDTH), BF16),
+            ((rows, WIDTH), BF16),
+            ((10,) + SLAB, BF16),
+            ((10,) + SLAB, BF16),
+        ),
+        (pltpu.VMEM((8, SHARD), F32),),
+    )
+    chunk_q, chunk_u = call(
+        merge_body, "merge", place, (keep, swap(send)), (((10,) + SLAB, BF16), ((8,) + SLAB, BF16))
+    )
+    (plane_q,) = call(zcat_q_body, "zcat_q", place, shifts(chunk_q), (((34,) + SLAB, BF16),))
+    q_parts = planes(plane_q)
+    same_core = planes(tok_sorted)
+    toks = tuple(t for part in same_core for t in (part, swap(part)))
+    cot_other = swap(cot_sorted)
+    (plane_u,) = call(zcat_u_body, "zcat_u", place, shifts(chunk_u), (((32,) + SLAB, BF16),))
+    u_parts = planes(plane_u)
+    (column_d,) = call(pcat_d_body, "pcat_d", place, down_parts, (((4, DOWN, WIDTH), BF16),))
+    d_parts = shifts(column_d)
+
+    heads = ((2, rows, HALF), BF16)
+    heads_all = ((8, rows, HALF), BF16)
+    wqkv, wo_mine, bias, q3, k3, v3, mixed3, mixed_low, lse = call(
+        functools.partial(attend_body, tables),
+        "attend",
+        place,
+        toks + q_parts,
+        (
+            ((WIDTH, 3 * HALF), BF16),
+            ((WIDTH, HALF), BF16),
+            ((SHARD, WIDTH), F32),
+            heads,
+            heads_all,
+            heads_all,
+            ((2, rows, HALF), F32),
+            heads,
+            ((2, rows, 128), F32),
+        ),
+        (
+            pltpu.VMEM((WIDTH, HALF), F32),
+            pltpu.VMEM((8, rows, WIDTH), BF16),
+            pltpu.VMEM((2, rows, HALF), BF16),
+            pltpu.VMEM((8, rows, HALF), BF16),
+            pltpu.VMEM((8, rows, HALF), BF16),
+        ),
+    )
+    pair = ((2, rows, WIDTH), BF16)
+    full = (2 * rows, WIDTH)
+    wide = ((2 * rows, 4 * HALF), BF16)
+    partial, vhat, scale, normed_low, active, slope, wup, wdown, mixed, wo = call(
+        forward_body,
+        "forward",
+        place,
+        (toks[0], toks[1], mixed_low, swap(mixed_low), wo_mine, swap(wo_mine), bias) + u_parts + d_parts,
+        (
+            pair,
+            (full, F32),
+            ((2 * rows, 1), F32),
+            (full, BF16),
+            wide,
+            wide,
+            ((WIDTH, 4 * HALF), BF16),
+            ((16, DOWN, WIDTH), BF16),
+            (full, BF16),
+            ((WIDTH, WIDTH), BF16),
+        ),
+        (pltpu.VMEM((WIDTH, HALF), F32), pltpu.VMEM(full, F32)),
+    )
+    layer_out, d_summed, d_down, d_upper, d_part, sums_ffn = call(
+        back_ffn_body,
+        "back_ffn",
+        place,
+        (perm, partial, swap(partial), vhat, bias, cot_sorted, cot_other, slope, wup, wdown),
+        (((rows, WIDTH), BF16), (full, F32), (full, BF16), wide, pair, ((8, WIDTH), F32)),
+    )
+    d_part_other = swap(d_part)
+    g_down = call(
+        grad_down_body,
+        "grad_down",
+        place,
+        (active, d_down),
+        (((4, DOWN, WIDTH), BF16),) * 4,
+        (pltpu.VMEM((4 * HALF, WIDTH), F32),),
+    )
+    g_down = (g_down[0],) + tuple(shift(g_down[k], k) for k in (1, 2, 3))
+    g_up = call(
+        grad_up_body,
+        "grad_up",
+        place,
+        (normed_low, d_upper),
+        (((32,) + SLAB, BF16),) * 4,
+        (pltpu.VMEM((WIDTH, HALF), F32),),
+    )
+    g_up = (g_up[0],) + tuple(plane(g_up[r], r) for r in (1, 2, 3))
+    d_hidden, d_branch, dq, dk, dv, sums_attn = call(
+        functools.partial(back_attend_body, tables),
+        "back_attend",
+        place,
+        (d_summed, d_part, d_part_other, vhat, scale, bias, wo, mixed3, q3, k3, v3, lse),
+        (((rows, WIDTH), F32), (full, BF16), heads, heads_all, heads_all, ((8, WIDTH), F32)),
+        (pltpu.VMEM((2, rows, HALF), BF16),),
+    )
+    g_q = call(
+        grad_qkvo_body,
+        "grad_qkvo",
+        place,
+        toks + (dq, dk, dv, mixed, d_branch, sums_ffn, sums_attn),
+        (((34,) + SLAB, BF16),) * 4,
+        (
+            pltpu.VMEM((WIDTH, HALF), F32),
+            pltpu.VMEM((8 * rows, WIDTH), BF16),
+            pltpu.VMEM((SHARD, WIDTH), F32),
+        ),
+    )
+    g_q = (g_q[0],) + tuple(plane(g_q[r], r) for r in (1, 2, 3))
+    quad = ((4, rows, WIDTH), BF16)
+    same, sib = call(grad_tok_body, "grad_tok", place, (dq, dk, dv, wqkv), (quad, quad))
+    s_tok = call(sum_tok_body, "sum_tok", place, (same, swap(sib)), (((rows, WIDTH), BF16),) * 4)
+    s_tok = (s_tok[0],) + tuple(plane(s_tok[r], r) for r in (1, 2, 3))
+
+    s_up = call(
+        functools.partial(sum_plane_body, False), "sum_up", place, g_up, (((8,) + SLAB, BF16),) * 4
+    )
+    s_up = (s_up[0],) + tuple(shift(s_up[k], k) for k in (1, 2, 3))
+    s_down = call(sum_down_body, "sum_down", place, g_down, (((DOWN, WIDTH), BF16),) * 4)
+    s_down = (s_down[0],) + tuple(plane(s_down[r], r) for r in (1, 2, 3))
+    s_q = call(
+        functools.partial(sum_plane_body, True), "sum_q", place, g_q, (((10,) + SLAB, BF16),) * 4
+    )
+    s_q = (s_q[0],) + tuple(shift(s_q[k], k) for k in (1, 2, 3))
+    (grad_tokens,) = call(
+        last_tok_body, "last_tok", place, (perm, d_hidden) + s_tok, (((rows, WIDTH), F32),)
+    )
+    (grad_down,) = call(last_down_body, "last_down", place, s_down, (((DOWN, WIDTH), F32),))
+    kept, sent = call(
+        sum_last_body, "sum_last", place, s_q + s_up, (((10,) + SLAB, F32), ((10,) + SLAB, F32))
+    )
+    row = ((SHARD, WIDTH), F32)
+    gq, gk, gv, go, gup, small, ups = call(
+        last_body,
+        "last",
+        place,
+        (kept, swap(sent)),
+        (row, row, row, row, ((SHARD, 4 * WIDTH), F32), ((SHARD, 128), F32), ((8, 128), F32)),
+    )
+    small = small[:, :SHARD]
+    return (
+        layer_out,
+        grad_tokens,
+        gq,
+        gk,
+        gv,
+        go,
+        gup,
+        grad_down,
+        small[0],
+        small[1],
+        small[2],
+        ups[0, :DOWN],
+        small[3],
+        small[4],
+        small[5],
+        small[6],
+        small[7],
+    )
+
+
 def solution(mesh):
     placed = (
         P(("col", "seq"), None),
@@ -345,8 +1097,9 @@
         P(("col", "seq")),
         P(("col", "seq"), None),
     )
+    fast = mesh.shape["col"] == 8 and mesh.shape["seq"] == 4
     return jax.shard_map(
-        per_device,
+        fast_device if fast else per_device,
         mesh=mesh,
         in_specs=placed,
         out_specs=(

time: 1340 us -> 367 us (0.27)
  waiting for transfers between devices: 965 us -> 138 us
  matrix products: 146 us -> 0 us
  Pallas kernels: 0 us -> 114 us
  starting transfers between devices: 0.81 us -> 93.2 us
  blocking collectives: 91.9 us -> 0 us
  local copies, waits for them, and re-layouts: 74.3 us -> 13.2 us
  other arithmetic: 38.6 us -> 0.61 us
    reduce_scatter x5 -> x0, waiting for transfers between devices: 397 us -> none  [the longest x1 142 us: per_device(): lax.psum_scatter(sums_local[5], ('col', 'seq'), scatter_dimension=0, tile...]
    unnamed x19 -> x0, waiting for transfers between devices: 317 us -> none
    all_gather x8 -> x0, waiting for transfers between devices: 251 us -> none  [the longest x1 53.1 us: per_device(): lax.all_gather(shards[5], ('col', 'seq'), axis=0, tiled=True)]
    dot_general x46 -> x0, matrix products: 146 us -> none  [the longest x5 23.2 us: project(): jnp.dot(left, right, preferred_element_type=FULL_TYPE)]
    ppermute x0 -> x54, waiting for transfers between devices: none -> 138 us  [the longest x24 83 us: plane(): return lax.ppermute(x, 'col', [(i, i ^ 2 * r) for i in range(8)])]
    pallas_call x0 -> x21, Pallas kernels: none -> 114 us  [call(): pl.pallas_call(body, name=name, out_shape=tuple((jax.ShapeDtypeStruct(s,...]
    ppermute x0 -> x54, starting transfers between devices: none -> 93.2 us  [the longest x18 62.6 us: shift(): return lax.ppermute(x, 'seq', [(i, (i + k) % 4) for i in range(4)])]
    unnamed x2 -> x0, blocking collectives: 82.9 us -> none
  transfers between devices with their start and end apart: 16 -> 54, of which waited for: 15 -> 18; matrix products, arithmetic and copies ran while one was open for 12% -> 1% of each run, Pallas kernels for 0% -> 16%
where the time goes in v1:
time: 367 us; the launch traced here: 361 us
  waiting for transfers between devices  138 us (38%)
  Pallas kernels  114 us (31%)
  starting transfers between devices  93.2 us (25%)
  local copies, waits for them, and re-layouts  13.2 us (4%)
    pallas_call x21, Pallas kernels, call(): pl.pallas_call(body, name=name, out_shape=tuple((jax.ShapeDtypeStruct(s,...  114 us
    ppermute x24, waiting for transfers between devices, plane(): return lax.ppermute(x, 'col', [(i, i ^ 2 * r) for i in range(8)])  83 us
    ppermute x18, starting transfers between devices, shift(): return lax.ppermute(x, 'seq', [(i, (i + k) % 4) for i in range(4)])  62.6 us
    ppermute x18, waiting for transfers between devices, shift(): return lax.ppermute(x, 'seq', [(i, (i + k) % 4) for i in range(4)])  50.3 us
    ppermute x24, starting transfers between devices, plane(): return lax.ppermute(x, 'col', [(i, i ^ 2 * r) for i in range(8)])  27.9 us
    unnamed x92, local copies, waits for them, and re-layouts  10.5 us
  transfers between devices with their start and end apart: 54, of which 18 were waited for; matrix products, arithmetic and copies ran while one was open for 1% of the time, Pallas kernels for 16%

profile of v1, /device:TPU:0, one launch (start us, length us, event | category | flops | bytes accessed | tf_op | source)
XLA Modules:
  0.0 360.5 jit_solution(3695603590103302292)
XLA Ops:
  1.3 2.9 prep.1
  4.7 2.5 collective-permute-start.22
  11.3 2.0 collective-permute-start.16
  13.3 2.6 collective-permute-start.17
  17.4 2.8 collective-permute-start.10
  23.0 2.6 collective-permute-done.17.r2
  25.6 3.4 collective-permute-start.8
  29.0 3.1 collective-permute-start.9
  32.1 5.1 %collective-permute-done.8.r1 = bf16[10,24,384]{2,1,0:T(8,128)(2,1)S(1)} collective-permute-done((bf16[10,24,384]{2,1,0:T(8,128)(2,1)}, bf16[10,24,384]{2,1,0:T(8,128)(2,1)S(1)}, u32[]{:S(2)}, u32[]{:S(2)}) %collective-permute-start.8) | collective-permute-done | bytes 184352 | tf_op jit(solution)/shard_map/ppermute | solution.py:893
  38.4 4.7 %collective-permute-done.9.r2 = bf16[10,24,384]{2,1,0:T(8,128)(2,1)S(1)} collective-permute-done((bf16[10,24,384]{2,1,0:T(8,128)(2,1)}, bf16[10,24,384]{2,1,0:T(8,128)(2,1)S(1)}, u32[]{:S(2)}, u32[]{:S(2)}) %collective-permute-start.9) | collective-permute-done | bytes 184352 | tf_op jit(solution)/shard_map/ppermute | solution.py:893
  43.8 2.2 zcat_q.1.refs_8_
  50.0 2.0 pcat_d.1.refs_4_
  52.8 3.3 collective-permute-start.26
  56.0 7.1 %collective-permute-done.11.refs_9_ = bf16[34,24,384]{2,1,0:T(8,128)(2,1)S(1)} collective-permute-done((bf16[34,24,384]{2,1,0:T(8,128)(2,1)}, bf16[34,24,384]{2,1,0:T(8,128)(2,1)S(1)}, u32[]{:S(2)}, u32[]{:S(2)}) %collective-permute-start.11) | collective-permute-done | bytes 626720 | tf_op jit(solution)/shard_map/ppermute | solution.py:890
  63.1 3.5 collective-permute-start.27
  66.6 2.0 zcat_u.1.refs_0_
  68.6 9.2 %collective-permute-done.12.refs_10_ = bf16[34,24,384]{2,1,0:T(8,128)(2,1)} collective-permute-done((bf16[34,24,384]{2,1,0:T(8,128)(2,1)}, bf16[34,24,384]{2,1,0:T(8,128)(2,1)}, u32[]{:S(2)}, u32[]{:S(2)}) %collective-permute-start.12) | collective-permute-done | bytes 626720 | tf_op jit(solution)/shard_map/ppermute | solution.py:890
  79.9 16.8 %attend.1 = (bf16[768,1152]{1,0:T(8,128)(2,1)}, bf16[768,384]{1,0:T(8,128)(2,1)}, f32[24,768]{1,0:T(8,128)}, bf16[2,256,384]{2,1,0:T(8,128)(2,1)}, bf16[8,256,38...) custom-call(s32[4]{0:T(128)} %pad_add_fusion.place, ...), custom_call_target="tpu_custom_call" | custom-call | bytes 13066240 | tf_op jit(solution)/shard_map/attend/pallas_call | solution.py:358
  98.7 12.9 %collective-permute-done.21.refs_3_ = bf16[32,24,384]{2,1,0:T(8,128)(2,1)S(1)} collective-permute-done((bf16[32,24,384]{2,1,0:T(8,128)(2,1)S(1)}, bf16[32,24,384]{2,1,0:T(8,128)(2,1)S(1)}, u32[]{:S(2)}, u32[]{:S(2)}) %collective-permute-start.21) | collective-permute-done | bytes 589856 | tf_op jit(solution)/shard_map/ppermute | solution.py:890
  112.8 12.9 %forward.1 = (bf16[2,256,768]{2,1,0:T(8,128)(2,1)}, f32[512,768]{1,0:T(8,128)}, f32[512,1]{1,0:T(8,128)}, bf16[512,768]{1,0:T(8,128)(2,1)}, bf16[512,1536]{1,0:T...) custom-call(s32[4]{0:T(128)} %pad_add_fusion.place, ...), custom_call_target="tpu_custom_call" | custom-call | bytes 20523008 | tf_op jit(solution)/shard_map/forward/pallas_call | solution.py:358
  126.3 2.3 collective-permute-done.29.cot1
  129.8 9.5 %back_ffn.1 = (bf16[256,768]{1,0:T(8,128)(2,1)}, f32[512,768]{1,0:T(8,128)}, bf16[512,768]{1,0:T(8,128)(2,1)}, bf16[512,1536]{1,0:T(8,128)(2,1)}, bf16[2,256,768]{2,1,0:T(8,128)(2,1)}, /*index=5*/f32[8,768]{1,0:T(8,128)}) custom-call(s32[4]{0:T(128)} %pad_add_fusion.place, bf16[256,256]{1,0:T(8,128)(2,1)} %get-tuple-element.94.perm, ...), custom_call_target="tpu_custom_call" | custom-call | bytes 15564800 | tf_op jit(solution)/shard_map/back_ffn/pallas_call | solution.py:358
  139.4 2.4 collective-permute-done.30.other
  142.7 16.5 %back_attend.1 = (f32[256,768]{1,0:T(8,128)}, bf16[512,768]{1,0:T(8,128)(2,1)}, bf16[2,256,384]{2,1,0:T(8,128)(2,1)}, bf16[8,256,384]{2,1,0:T(8,128)(2,1)}, bf16...) custom-call(s32[4]{0:T(128)} %pad_add_fusion.place, f32[512,768]{1,0:T(8,128)} %get-tuple-element.110.d_summed, ...), custom_call_target="tpu_custom_call" | custom-call | bytes 15697920 | tf_op jit(solution)/shard_map/back_attend/pallas_call | solution.py:358
  159.2 9.5 %grad_qkvo.1 = (bf16[34,24,384]{2,1,0:T(8,128)(2,1)}, bf16[34,24,384]{2,1,0:T(8,128)(2,1)}, bf16[34,24,384]{2,1,0:T(8,128)(2,1)}, bf16[34,24,384]{2,1,0:T(8,128)(2,1)}) custom-call(s32[4]{0:T(128)} %pad_add_fusion.place, bf16[256,768]{1,0:T(8,128)(2,1)} %get-tuple-element.95.refs_0_.tok0, bf16[256,768]{1,0:T(8,128)(2,1)} %copy-done, ...), custom_call_target="tpu_custom_call" | custom-call | bytes 10813440 | tf_op jit(solution)/shard_map/grad_qkvo/pallas_call | solution.py:358
  170.6 7.7 %grad_tok.1 = (bf16[4,256,768]{2,1,0:T(8,128)(2,1)}, bf16[4,256,768]{2,1,0:T(8,128)(2,1)}) custom-call(s32[4]{0:T(128)} %pad_add_fusion.place, bf16[2,256,384]{2,1,0:T(8,128)(2,1)} %get-tuple-element.120.dq.refs_8_, bf16[8,256,384]{2,1,0:T(8,128)(2,1)} %get-tuple-element.121.dk.refs_9_, bf16[8,256,384]{2,1,0:T(8,128)(2,1)} %get-tuple-element.122.dv.refs_10_, ...), custom_call_target="tpu_custom_call" | custom-call | bytes 8454144 | tf_op jit(solution)/shard_map/grad_tok/pallas_call | solution.py:358
  179.9 4.9 %grad_up.1 = (bf16[32,24,384]{2,1,0:T(8,128)(2,1)}, bf16[32,24,384]{2,1,0:T(8,128)(2,1)}, bf16[32,24,384]{2,1,0:T(8,128)(2,1)}, bf16[32,24,384]{2,1,0:T(8,128)(2,1)}) custom-call(s32[4]{0:T(128)} %pad_add_fusion.place, bf16[512,768]{1,0:T(8,128)(2,1)} %get-tuple-element.142.normed_low, bf16[512,1536]{1,0:T(8,128)(2,1)} %get-tuple-element.143.d_upper), custom_call_target="tpu_custom_call" | custom-call | bytes 4718592 | tf_op jit(solution)/shard_map/grad_up/pallas_call | solution.py:358
  186.7 14.0 %collective-permute-done.36.r2 = bf16[34,24,384]{2,1,0:T(8,128)(2,1)S(1)} collective-permute-done((bf16[34,24,384]{2,1,0:T(8,128)(2,1)}, bf16[34,24,384]{2,1,0:T(8,128)(2,1)S(1)}, u32[]{:S(2)}, u32[]{:S(2)}) %collective-permute-start.36) | collective-permute-done | bytes 626720 | tf_op jit(solution)/shard_map/ppermute | solution.py:890
  201.8 2.7 sum_q.1
  205.5 6.5 %collective-permute-done.41.r1 = bf16[32,24,384]{2,1,0:T(8,128)(2,1)S(1)} collective-permute-done((bf16[32,24,384]{2,1,0:T(8,128)(2,1)}, bf16[32,24,384]{2,1,0:T(8,128)(2,1)S(1)}, u32[]{:S(2)}, u32[]{:S(2)}) %collective-permute-start.41) | collective-permute-done | bytes 589856 | tf_op jit(solution)/shard_map/ppermute | solution.py:890
  212.0 13.1 %collective-permute-done.42.r2 = bf16[32,24,384]{2,1,0:T(8,128)(2,1)} collective-permute-done((bf16[32,24,384]{2,1,0:T(8,128)(2,1)}, bf16[32,24,384]{2,1,0:T(8,128)(2,1)}, u32[]{:S(2)}, u32[]{:S(2)}) %collective-permute-start.42) | collective-permute-done | bytes 589856 | tf_op jit(solution)/shard_map/ppermute | solution.py:890
  225.0 2.6 sum_up.1
  228.4 3.3 collective-permute-start.45
  232.1 4.5 %grad_down.1 = (bf16[4,96,768]{2,1,0:T(8,128)(2,1)}, bf16[4,96,768]{2,1,0:T(8,128)(2,1)}, bf16[4,96,768]{2,1,0:T(8,128)(2,1)}, bf16[4,96,768]{2,1,0:T(8,128)(2,1)}) custom-call(s32[4]{0:T(128)} %pad_add_fusion.place, bf16[512,1536]{1,0:T(8,128)(2,1)} %get-tuple-element.159.active, bf16[512,768]{1,0:T(8,128)(2,1)} %get-tuple-element.160.d_down), custom_call_target="tpu_custom_call" | custom-call | bytes 4718592 | tf_op jit(solution)/shard_map/grad_down/pallas_call | solution.py:358
  236.7 4.0 %collective-permute-start.48 = (bf16[4,96,768]{2,1,0:T(8,128)(2,1)}, bf16[4,96,768]{2,1,0:T(8,128)(2,1)S(1)}, u32[]{:S(2)}, u32[]{:S(2)}) collective-permute-start(bf16[4,96,768]{2,1,0:T(8,128)(2,1)} %get-tuple-element.162), channel_id=1, source_target_pairs={{0,1},{1,2},{2,3},{3,0},{4,5},{5,6},{6,7},{7,4},{8,9},{9,10},{10,1... | collective-permute-start | bytes 1769480 | tf_op jit(solution)/shard_map/ppermute | solution.py:893
  242.6 4.0 %collective-permute-start.50 = (bf16[4,96,768]{2,1,0:T(8,128)(2,1)}, bf16[4,96,768]{2,1,0:T(8,128)(2,1)S(1)}, u32[]{:S(2)}, u32[]{:S(2)}) collective-permute-start(bf16[4,96,768]{2,1,0:T(8,128)(2,1)} %get-tuple-element.164), channel_id=1, source_target_pairs={{0,3},{1,0},{2,1},{3,2},{4,7},{5,4},{6,5},{7,6},{8,11},{9,8},{10,9... | collective-permute-start | bytes 1769480 | tf_op jit(solution)/shard_map/ppermute | solution.py:893
  246.6 24.7 %collective-permute-start.39 = (bf16[10,24,384]{2,1,0:T(8,128)(2,1)}, bf16[10,24,384]{2,1,0:T(8,128)(2,1)S(1)}, u32[]{:S(2)}, u32[]{:S(2)}) collective-permute-start(bf16[10,24,384]{2,1,0:T(8,128)(2,1)} %get-tuple-element.140), channel_id=1, source_target_pairs={{0,2},{1,3},{2,0},{3,1},{4,6},{5,7},{6,4},{7,5},{8,10},{9,11},{10,... | collective-permute-start | bytes 552968 | tf_op jit(solution)/shard_map/ppermute | solution.py:893
  271.3 31.0 %collective-permute-done.39.q2 = bf16[10,24,384]{2,1,0:T(8,128)(2,1)S(1)} collective-permute-done((bf16[10,24,384]{2,1,0:T(8,128)(2,1)}, bf16[10,24,384]{2,1,0:T(8,128)(2,1)S(1)}, u32[]{:S(2)}, u32[]{:S(2)}) %collective-permute-start.39) | collective-permute-done | bytes 184352 | tf_op jit(solution)/shard_map/ppermute | solution.py:893
  303.4 5.7 %collective-permute-done.40.q3 = bf16[10,24,384]{2,1,0:T(8,128)(2,1)S(1)} collective-permute-done((bf16[10,24,384]{2,1,0:T(8,128)(2,1)}, bf16[10,24,384]{2,1,0:T(8,128)(2,1)S(1)}, u32[]{:S(2)}, u32[]{:S(2)}) %collective-permute-start.40) | collective-permute-done | bytes 184352 | tf_op jit(solution)/shard_map/ppermute | solution.py:893
  309.8 2.4 sum_last.1
  313.5 2.6 sum_down.1
  319.5 3.4 collective-permute-done.51.r1
  322.9 4.0 %collective-permute-done.52.r2 = bf16[96,768]{1,0:T(8,128)(2,1)S(1)} collective-permute-done((bf16[96,768]{1,0:T(8,128)(2,1)}, bf16[96,768]{1,0:T(8,128)(2,1)S(1)}, u32[]{:S(2)}, u32[]{:S(2)}) %collective-permute-start.52) | collective-permute-done | bytes 147488 | tf_op jit(solution)/shard_map/ppermute | solution.py:890
  330.3 2.3 last.1
  333.7 3.1 sum_tok.1
  343.0 6.1 %collective-permute-done.32.r1 = bf16[256,768]{1,0:T(8,128)(2,1)S(1)} collective-permute-done((bf16[256,768]{1,0:T(8,128)(2,1)}, bf16[256,768]{1,0:T(8,128)(2,1)S(1)}, u32[]{:S(2)}, u32[]{:S(2)}) %collective-permute-start.32) | collective-permute-done | bytes 393248 | tf_op jit(solution)/shard_map/ppermute | solution.py:890
  349.1 6.9 %collective-permute-done.33.r2 = bf16[256,768]{1,0:T(8,128)(2,1)S(1)} collective-permute-done((bf16[256,768]{1,0:T(8,128)(2,1)}, bf16[256,768]{1,0:T(8,128)(2,1)S(1)}, u32[]{:S(2)}, u32[]{:S(2)}) %collective-permute-start.33) | collective-permute-done | bytes 393248 | tf_op jit(solution)/shard_map/ppermute | solution.py:890
  356.9 3.2 last_tok.1
  (176 shorter events, 52.8 us)
Async XLA Ops:
  4.7 11.2 %collective-permute-start.22 = (bf16[96,768]{1,0:T(8,128)(2,1)}, bf16[96,768]{1,0:T(8,128)(2,1)S(1)}, u32[]{:S(2)}, u32[]{:S(2)}) collective-permute-start(bf16[96,768]{1,0:T(8,128)(2,1)} %own.1), channel_id=1, source_target_pairs={{0,8},{4,12},{8,0},{12,4},{16,24},{20,28},{24,16},{28,20},{1,9},{5... | collective-permute-start | bytes 442376 | tf_op jit(solution)/shard_map/ppermute | solution.py:890
  7.2 10.1 %collective-permute-start.23 = (bf16[96,768]{1,0:T(8,128)(2,1)}, bf16[96,768]{1,0:T(8,128)(2,1)S(1)}, u32[]{:S(2)}, u32[]{:S(2)}) collective-permute-start(bf16[96,768]{1,0:T(8,128)(2,1)} %own.1), channel_id=1, source_target_pairs={{0,16},{4,20},{8,24},{12,28},{16,0},{20,4},{24,8},{28,12},{1,17},{... | collective-permute-start | bytes 442376 | tf_op jit(solution)/shard_map/ppermute | solution.py:890
  8.8 11.4 %collective-permute-start.24 = (bf16[96,768]{1,0:T(8,128)(2,1)}, bf16[96,768]{1,0:T(8,128)(2,1)S(1)}, u32[]{:S(2)}, u32[]{:S(2)}) collective-permute-start(bf16[96,768]{1,0:T(8,128)(2,1)} %own.1), channel_id=1, source_target_pairs={{0,24},{4,28},{8,16},{12,20},{16,8},{20,12},{24,0},{28,4},{1,25},{... | collective-permute-start | bytes 442376 | tf_op jit(solution)/shard_map/ppermute | solution.py:890
  11.3 10.4 %collective-permute-start.16 = (bf16[8,24,384]{2,1,0:T(8,128)(2,1)}, bf16[8,24,384]{2,1,0:T(8,128)(2,1)S(1)}, u32[]{:S(2)}, u32[]{:S(2)}) collective-permute-start(bf16[8,24,384]{2,1,0:T(8,128)(2,1)} %get-tuple-element.102.own), channel_id=1, source_target_pairs={{0,1},{1,2},{2,3},{3,0},{4,5},{5,6},{6,7},{7,4},{8,9},{9,10},{10,1... | collective-permute-start | bytes 442376 | tf_op jit(solution)/shard_map/ppermute | solution.py:893
  13.3 12.3 %collective-permute-start.17 = (bf16[8,24,384]{2,1,0:T(8,128)(2,1)}, bf16[8,24,384]{2,1,0:T(8,128)(2,1)S(1)}, u32[]{:S(2)}, u32[]{:S(2)}) collective-permute-start(bf16[8,24,384]{2,1,0:T(8,128)(2,1)} %get-tuple-element.102.own), channel_id=1, source_target_pairs={{0,2},{1,3},{2,0},{3,1},{4,6},{5,7},{6,4},{7,5},{8,10},{9,11},{10,... | collective-permute-start | bytes 442376 | tf_op jit(solution)/shard_map/ppermute | solution.py:893
  15.9 27.2 %collective-permute-start.1 = (bf16[256,768]{1,0:T(8,128)(2,1)}, bf16[256,768]{1,0:T(8,128)(2,1)S(1)}, u32[]{:S(2)}, u32[]{:S(2)}) collective-permute-start(bf16[256,768]{1,0:T(8,128)(2,1)} %get-tuple-element.95.refs_0_.tok0), channel_id=1, source_target_pairs={{0,8},{4,12},{8,0},{12,4},{16,24},{20,28},{24,16},{28,20},{1,9},{5... | collective-permute-start | bytes 1179656 | tf_op jit(solution)/shard_map/ppermute | solution.py:890
  17.4 11.7 %collective-permute-start.10 = (bf16[10,24,384]{2,1,0:T(8,128)(2,1)}, bf16[10,24,384]{2,1,0:T(8,128)(2,1)S(1)}, u32[]{:S(2)}, u32[]{:S(2)}) collective-permute-start(bf16[10,24,384]{2,1,0:T(8,128)(2,1)} %get-tuple-element.98.own), channel_id=1, source_target_pairs={{0,3},{1,0},{2,1},{3,2},{4,7},{5,4},{6,5},{7,6},{8,11},{9,8},{10,9... | collective-permute-start | bytes 552968 | tf_op jit(solution)/shard_map/ppermute | solution.py:893
  20.1 27.3 %collective-permute-start.3 = (bf16[256,768]{1,0:T(8,128)(2,1)}, bf16[256,768]{1,0:T(8,128)(2,1)S(1)}, u32[]{:S(2)}, u32[]{:S(2)}) collective-permute-start(bf16[256,768]{1,0:T(8,128)(2,1)} %get-tuple-element.95.refs_0_.tok0), channel_id=1, source_target_pairs={{0,16},{4,20},{8,24},{12,28},{16,0},{20,4},{24,8},{28,12},{1,17},{... | collective-permute-start | bytes 1179656 | tf_op jit(solution)/shard_map/ppermute | solution.py:890
  21.7 25.8 %collective-permute-start.5 = (bf16[256,768]{1,0:T(8,128)(2,1)}, bf16[256,768]{1,0:T(8,128)(2,1)S(1)}, u32[]{:S(2)}, u32[]{:S(2)}) collective-permute-start(bf16[256,768]{1,0:T(8,128)(2,1)} %get-tuple-element.95.refs_0_.tok0), channel_id=1, source_target_pairs={{0,24},{4,28},{8,16},{12,20},{16,8},{20,12},{24,0},{28,4},{1,25},{... | collective-permute-start | bytes 1179656 | tf_op jit(solution)/shard_map/ppermute | solution.py:890
  25.6 11.6 %collective-permute-start.8 = (bf16[10,24,384]{2,1,0:T(8,128)(2,1)}, bf16[10,24,384]{2,1,0:T(8,128)(2,1)S(1)}, u32[]{:S(2)}, u32[]{:S(2)}) collective-permute-start(bf16[10,24,384]{2,1,0:T(8,128)(2,1)} %get-tuple-element.98.own), channel_id=1, source_target_pairs={{0,1},{1,2},{2,3},{3,0},{4,5},{5,6},{6,7},{7,4},{8,9},{9,10},{10,1... | collective-permute-start | bytes 552968 | tf_op jit(solution)/shard_map/ppermute | solution.py:893
  29.0 14.1 %collective-permute-start.9 = (bf16[10,24,384]{2,1,0:T(8,128)(2,1)}, bf16[10,24,384]{2,1,0:T(8,128)(2,1)S(1)}, u32[]{:S(2)}, u32[]{:S(2)}) collective-permute-start(bf16[10,24,384]{2,1,0:T(8,128)(2,1)} %get-tuple-element.98.own), channel_id=1, source_target_pairs={{0,2},{1,3},{2,0},{3,1},{4,6},{5,7},{6,4},{7,5},{8,10},{9,11},{10,... | collective-permute-start | bytes 552968 | tf_op jit(solution)/shard_map/ppermute | solution.py:893
  37.2 8.7 %collective-permute-start.18 = (bf16[8,24,384]{2,1,0:T(8,128)(2,1)}, bf16[8,24,384]{2,1,0:T(8,128)(2,1)}, u32[]{:S(2)}, u32[]{:S(2)}) collective-permute-start(bf16[8,24,384]{2,1,0:T(8,128)(2,1)} %get-tuple-element.102.own), channel_id=1, source_target_pairs={{0,3},{1,0},{2,1},{3,2},{4,7},{5,4},{6,5},{7,6},{8,11},{9,8},{10,9... | collective-permute-start | bytes 442376 | tf_op jit(solution)/shard_map/ppermute | solution.py:893
  43.1 6.4 %collective-permute-start.2 = (bf16[256,768]{1,0:T(8,128)(2,1)S(1)}, bf16[256,768]{1,0:T(8,128)(2,1)S(1)}, u32[]{:S(2)}, u32[]{:S(2)}) collective-permute-start(bf16[256,768]{1,0:T(8,128)(2,1)S(1)} %collective-permute-done.1.refs_2_), channel_id=1, source_target_pairs={{0,4},{4,0},{8,12},{12,8},{16,20},{20,16},{24,28},{28,24},{1,5},{5... | collective-permute-start | bytes 1179656 | tf_op jit(solution)/shard_map/ppermute | solution.py:887
  45.9 17.2 %collective-permute-start.11 = (bf16[34,24,384]{2,1,0:T(8,128)(2,1)}, bf16[34,24,384]{2,1,0:T(8,128)(2,1)S(1)}, u32[]{:S(2)}, u32[]{:S(2)}) collective-permute-start(bf16[34,24,384]{2,1,0:T(8,128)(2,1)} %zcat_q.1.refs_8_), channel_id=1, source_target_pairs={{0,8},{4,12},{8,0},{12,4},{16,24},{20,28},{24,16},{28,20},{1,9},{5... | collective-permute-start | bytes 1880072 | tf_op jit(solution)/shard_map/ppermute | solution.py:890
  47.5 5.3 %collective-permute-start.6 = (bf16[256,768]{1,0:T(8,128)(2,1)S(1)}, bf16[256,768]{1,0:T(8,128)(2,1)S(1)}, u32[]{:S(2)}, u32[]{:S(2)}) collective-permute-start(bf16[256,768]{1,0:T(8,128)(2,1)S(1)} %collective-permute-done.5.refs_6_), channel_id=1, source_target_pairs={{0,4},{4,0},{8,12},{12,8},{16,20},{20,16},{24,28},{28,24},{1,5},{5... | collective-permute-start | bytes 1179656 | tf_op jit(solution)/shard_map/ppermute | solution.py:887
  47.9 29.9 %collective-permute-start.12 = (bf16[34,24,384]{2,1,0:T(8,128)(2,1)}, bf16[34,24,384]{2,1,0:T(8,128)(2,1)}, u32[]{:S(2)}, u32[]{:S(2)}) collective-permute-start(bf16[34,24,384]{2,1,0:T(8,128)(2,1)} %zcat_q.1.refs_8_), channel_id=1, source_target_pairs={{0,16},{4,20},{8,24},{12,28},{16,0},{20,4},{24,8},{28,12},{1,17},{... | collective-permute-start | bytes 1880072 | tf_op jit(solution)/shard_map/ppermute | solution.py:890
  49.5 28.9 %collective-permute-start.13 = (bf16[34,24,384]{2,1,0:T(8,128)(2,1)}, bf16[34,24,384]{2,1,0:T(8,128)(2,1)}, u32[]{:S(2)}, u32[]{:S(2)}) collective-permute-start(bf16[34,24,384]{2,1,0:T(8,128)(2,1)} %zcat_q.1.refs_8_), channel_id=1, source_target_pairs={{0,24},{4,28},{8,16},{12,20},{16,8},{20,12},{24,0},{28,4},{1,25},{... | collective-permute-start | bytes 1880072 | tf_op jit(solution)/shard_map/ppermute | solution.py:890
  52.0 44.7 %collective-permute-start.25 = (bf16[4,96,768]{2,1,0:T(8,128)(2,1)}, bf16[4,96,768]{2,1,0:T(8,128)(2,1)}, u32[]{:S(2)}, u32[]{:S(2)}) collective-permute-start(bf16[4,96,768]{2,1,0:T(8,128)(2,1)} %pcat_d.1.refs_4_), channel_id=1, source_target_pairs={{0,1},{1,2},{2,3},{3,0},{4,5},{5,6},{6,7},{7,4},{8,9},{9,10},{10,1... | collective-permute-start | bytes 1769480 | tf_op jit(solution)/shard_map/ppermute | solution.py:893
  52.8 45.4 %collective-permute-start.26 = (bf16[4,96,768]{2,1,0:T(8,128)(2,1)}, bf16[4,96,768]{2,1,0:T(8,128)(2,1)}, u32[]{:S(2)}, u32[]{:S(2)}) collective-permute-start(bf16[4,96,768]{2,1,0:T(8,128)(2,1)} %pcat_d.1.refs_4_), channel_id=1, source_target_pairs={{0,2},{1,3},{2,0},{3,1},{4,6},{5,7},{6,4},{7,5},{8,10},{9,11},{10,... | collective-permute-start | bytes 1769480 | tf_op jit(solution)/shard_map/ppermute | solution.py:893
  63.1 35.1 %collective-permute-start.27 = (bf16[4,96,768]{2,1,0:T(8,128)(2,1)}, bf16[4,96,768]{2,1,0:T(8,128)(2,1)}, u32[]{:S(2)}, u32[]{:S(2)}) collective-permute-start(bf16[4,96,768]{2,1,0:T(8,128)(2,1)} %pcat_d.1.refs_4_), channel_id=1, source_target_pairs={{0,3},{1,0},{2,1},{3,2},{4,7},{5,4},{6,5},{7,6},{8,11},{9,8},{10,9... | collective-permute-start | bytes 1769480 | tf_op jit(solution)/shard_map/ppermute | solution.py:893
  77.8 20.9 %collective-permute-start.19 = (bf16[32,24,384]{2,1,0:T(8,128)(2,1)}, bf16[32,24,384]{2,1,0:T(8,128)(2,1)}, u32[]{:S(2)}, u32[]{:S(2)}) collective-permute-start(bf16[32,24,384]{2,1,0:T(8,128)(2,1)} %zcat_u.1.refs_0_), channel_id=1, source_target_pairs={{0,8},{4,12},{8,0},{12,4},{16,24},{20,28},{24,16},{28,20},{1,9},{5... | collective-permute-start | bytes 1769480 | tf_op jit(solution)/shard_map/ppermute | solution.py:890
  78.3 20.4 %collective-permute-start.20 = (bf16[32,24,384]{2,1,0:T(8,128)(2,1)}, bf16[32,24,384]{2,1,0:T(8,128)(2,1)}, u32[]{:S(2)}, u32[]{:S(2)}) collective-permute-start(bf16[32,24,384]{2,1,0:T(8,128)(2,1)} %zcat_u.1.refs_0_), channel_id=1, source_target_pairs={{0,16},{4,20},{8,24},{12,28},{16,0},{20,4},{24,8},{28,12},{1,17},{... | collective-permute-start | bytes 1769480 | tf_op jit(solution)/shard_map/ppermute | solution.py:890
  96.7 14.9 %collective-permute-start.21 = (bf16[32,24,384]{2,1,0:T(8,128)(2,1)S(1)}, bf16[32,24,384]{2,1,0:T(8,128)(2,1)S(1)}, u32[]{:S(2)}, u32[]{:S(2)}) collective-permute-start(bf16[32,24,384]{2,1,0:T(8,128)(2,1)S(1)} %copy-done.1), channel_id=1, source_target_pairs={{0,24},{4,28},{8,16},{12,20},{16,8},{20,12},{24,0},{28,4},{1,25},{... | collective-permute-start | bytes 1769480 | tf_op jit(solution)/shard_map/ppermute | solution.py:890
  98.2 13.4 %collective-permute-start.15 = (bf16[768,384]{1,0:T(8,128)(2,1)}, bf16[768,384]{1,0:T(8,128)(2,1)S(1)}, u32[]{:S(2)}, u32[]{:S(2)}) collective-permute-start(bf16[768,384]{1,0:T(8,128)(2,1)} %get-tuple-element.100.wo_mine), channel_id=1, source_target_pairs={{0,4},{4,0},{8,12},{12,8},{16,20},{20,16},{24,28},{28,24},{1,5},{5... | collective-permute-start | bytes 1769480 | tf_op jit(solution)/shard_map/ppermute | solution.py:887
  98.2 13.4 %collective-permute-start.14 = (bf16[2,256,384]{2,1,0:T(8,128)(2,1)}, bf16[2,256,384]{2,1,0:T(8,128)(2,1)S(1)}, u32[]{:S(2)}, u32[]{:S(2)}) collective-permute-start(bf16[2,256,384]{2,1,0:T(8,128)(2,1)} %get-tuple-element.99.mine), channel_id=1, source_target_pairs={{0,4},{4,0},{8,12},{12,8},{16,20},{20,16},{24,28},{28,24},{1,5},{5... | collective-permute-start | bytes 1179656 | tf_op jit(solution)/shard_map/ppermute | solution.py:887
  168.7 17.6 %collective-permute-start.35 = (bf16[34,24,384]{2,1,0:T(8,128)(2,1)}, bf16[34,24,384]{2,1,0:T(8,128)(2,1)S(1)}, u32[]{:S(2)}, u32[]{:S(2)}) collective-permute-start(bf16[34,24,384]{2,1,0:T(8,128)(2,1)} %get-tuple-element.135), channel_id=1, source_target_pairs={{0,8},{4,12},{8,0},{12,4},{16,24},{20,28},{24,16},{28,20},{1,9},{5... | collective-permute-start | bytes 1880072 | tf_op jit(solution)/shard_map/ppermute | solution.py:890
  170.1 30.6 %collective-permute-start.36 = (bf16[34,24,384]{2,1,0:T(8,128)(2,1)}, bf16[34,24,384]{2,1,0:T(8,128)(2,1)S(1)}, u32[]{:S(2)}, u32[]{:S(2)}) collective-permute-start(bf16[34,24,384]{2,1,0:T(8,128)(2,1)} %get-tuple-element.136), channel_id=1, source_target_pairs={{0,16},{4,20},{8,24},{12,28},{16,0},{20,4},{24,8},{28,12},{1,17},{... | collective-permute-start | bytes 1880072 | tf_op jit(solution)/shard_map/ppermute | solution.py:890
  178.3 154.2 %collective-permute-start.31 = (bf16[4,256,768]{2,1,0:T(8,128)(2,1)}, bf16[4,256,768]{2,1,0:T(8,128)(2,1)S(1)}, u32[]{:S(2)}, u32[]{:S(2)}) collective-permute-start(bf16[4,256,768]{2,1,0:T(8,128)(2,1)} %get-tuple-element.125), channel_id=1, source_target_pairs={{0,4},{4,0},{8,12},{12,8},{16,20},{20,16},{24,28},{28,24},{1,5},{5... | collective-permute-start | bytes 4718600 | tf_op jit(solution)/shard_map/ppermute | solution.py:887
  178.3 22.4 %collective-permute-start.37 = (bf16[34,24,384]{2,1,0:T(8,128)(2,1)}, bf16[34,24,384]{2,1,0:T(8,128)(2,1)S(1)}, u32[]{:S(2)}, u32[]{:S(2)}) collective-permute-start(bf16[34,24,384]{2,1,0:T(8,128)(2,1)} %get-tuple-element.137), channel_id=1, source_target_pairs={{0,24},{4,28},{8,16},{12,20},{16,8},{20,12},{24,0},{28,4},{1,25},{... | collective-permute-start | bytes 1880072 | tf_op jit(solution)/shard_map/ppermute | solution.py:890
  184.8 27.2 %collective-permute-start.41 = (bf16[32,24,384]{2,1,0:T(8,128)(2,1)}, bf16[32,24,384]{2,1,0:T(8,128)(2,1)S(1)}, u32[]{:S(2)}, u32[]{:S(2)}) collective-permute-start(bf16[32,24,384]{2,1,0:T(8,128)(2,1)} %get-tuple-element.145), channel_id=1, source_target_pairs={{0,8},{4,12},{8,0},{12,4},{16,24},{20,28},{24,16},{28,20},{1,9},{5... | collective-permute-start | bytes 1769480 | tf_op jit(solution)/shard_map/ppermute | solution.py:890
  186.2 38.8 %collective-permute-start.42 = (bf16[32,24,384]{2,1,0:T(8,128)(2,1)}, bf16[32,24,384]{2,1,0:T(8,128)(2,1)}, u32[]{:S(2)}, u32[]{:S(2)}) collective-permute-start(bf16[32,24,384]{2,1,0:T(8,128)(2,1)} %get-tuple-element.146), channel_id=1, source_target_pairs={{0,16},{4,20},{8,24},{12,28},{16,0},{20,4},{24,8},{28,12},{1,17},{... | collective-permute-start | bytes 1769480 | tf_op jit(solution)/shard_map/ppermute | solution.py:890
  200.8 24.3 %collective-permute-start.43 = (bf16[32,24,384]{2,1,0:T(8,128)(2,1)}, bf16[32,24,384]{2,1,0:T(8,128)(2,1)}, u32[]{:S(2)}, u32[]{:S(2)}) collective-permute-start(bf16[32,24,384]{2,1,0:T(8,128)(2,1)} %get-tuple-element.147), channel_id=1, source_target_pairs={{0,24},{4,28},{8,16},{12,20},{16,8},{20,12},{24,0},{28,4},{1,25},{... | collective-permute-start | bytes 1769480 | tf_op jit(solution)/shard_map/ppermute | solution.py:890
  204.5 42.1 %collective-permute-start.38 = (bf16[10,24,384]{2,1,0:T(8,128)(2,1)}, bf16[10,24,384]{2,1,0:T(8,128)(2,1)S(1)}, u32[]{:S(2)}, u32[]{:S(2)}) collective-permute-start(bf16[10,24,384]{2,1,0:T(8,128)(2,1)} %get-tuple-element.139), channel_id=1, source_target_pairs={{0,1},{1,2},{2,3},{3,0},{4,5},{5,6},{6,7},{7,4},{8,9},{9,10},{10,1... | collective-permute-start | bytes 552968 | tf_op jit(solution)/shard_map/ppermute | solution.py:893
  227.6 9.1 %collective-permute-start.44 = (bf16[8,24,384]{2,1,0:T(8,128)(2,1)}, bf16[8,24,384]{2,1,0:T(8,128)(2,1)S(1)}, u32[]{:S(2)}, u32[]{:S(2)}) collective-permute-start(bf16[8,24,384]{2,1,0:T(8,128)(2,1)} %get-tuple-element.149), channel_id=1, source_target_pairs={{0,1},{1,2},{2,3},{3,0},{4,5},{5,6},{6,7},{7,4},{8,9},{9,10},{10,1... | collective-permute-start | bytes 442376 | tf_op jit(solution)/shard_map/ppermute | solution.py:893
  228.4 13.5 %collective-permute-start.45 = (bf16[8,24,384]{2,1,0:T(8,128)(2,1)}, bf16[8,24,384]{2,1,0:T(8,128)(2,1)S(1)}, u32[]{:S(2)}, u32[]{:S(2)}) collective-permute-start(bf16[8,24,384]{2,1,0:T(8,128)(2,1)} %get-tuple-element.150), channel_id=1, source_target_pairs={{0,2},{1,3},{2,0},{3,1},{4,6},{5,7},{6,4},{7,5},{8,10},{9,11},{10,... | collective-permute-start | bytes 442376 | tf_op jit(solution)/shard_map/ppermute | solution.py:893
  231.7 10.9 %collective-permute-start.46 = (bf16[8,24,384]{2,1,0:T(8,128)(2,1)}, bf16[8,24,384]{2,1,0:T(8,128)(2,1)S(1)}, u32[]{:S(2)}, u32[]{:S(2)}) collective-permute-start(bf16[8,24,384]{2,1,0:T(8,128)(2,1)} %get-tuple-element.151), channel_id=1, source_target_pairs={{0,3},{1,0},{2,1},{3,2},{4,7},{5,4},{6,5},{7,6},{8,11},{9,8},{10,9... | collective-permute-start | bytes 442376 | tf_op jit(solution)/shard_map/ppermute | solution.py:893
  236.7 75.5 %collective-permute-start.48 = (bf16[4,96,768]{2,1,0:T(8,128)(2,1)}, bf16[4,96,768]{2,1,0:T(8,128)(2,1)S(1)}, u32[]{:S(2)}, u32[]{:S(2)}) collective-permute-start(bf16[4,96,768]{2,1,0:T(8,128)(2,1)} %get-tuple-element.162), channel_id=1, source_target_pairs={{0,1},{1,2},{2,3},{3,0},{4,5},{5,6},{6,7},{7,4},{8,9},{9,10},{10,1... | collective-permute-start | bytes 1769480 | tf_op jit(solution)/shard_map/ppermute | solution.py:893
  241.8 70.4 %collective-permute-start.49 = (bf16[4,96,768]{2,1,0:T(8,128)(2,1)}, bf16[4,96,768]{2,1,0:T(8,128)(2,1)S(1)}, u32[]{:S(2)}, u32[]{:S(2)}) collective-permute-start(bf16[4,96,768]{2,1,0:T(8,128)(2,1)} %get-tuple-element.163), channel_id=1, source_target_pairs={{0,2},{1,3},{2,0},{3,1},{4,6},{5,7},{6,4},{7,5},{8,10},{9,11},{10,... | collective-permute-start | bytes 1769480 | tf_op jit(solution)/shard_map/ppermute | solution.py:893
  242.6 69.7 %collective-permute-start.50 = (bf16[4,96,768]{2,1,0:T(8,128)(2,1)}, bf16[4,96,768]{2,1,0:T(8,128)(2,1)S(1)}, u32[]{:S(2)}, u32[]{:S(2)}) collective-permute-start(bf16[4,96,768]{2,1,0:T(8,128)(2,1)} %get-tuple-element.164), channel_id=1, source_target_pairs={{0,3},{1,0},{2,1},{3,2},{4,7},{5,4},{6,5},{7,6},{8,11},{9,8},{10,9... | collective-permute-start | bytes 1769480 | tf_op jit(solution)/shard_map/ppermute | solution.py:893
  246.6 55.7 %collective-permute-start.39 = (bf16[10,24,384]{2,1,0:T(8,128)(2,1)}, bf16[10,24,384]{2,1,0:T(8,128)(2,1)S(1)}, u32[]{:S(2)}, u32[]{:S(2)}) collective-permute-start(bf16[10,24,384]{2,1,0:T(8,128)(2,1)} %get-tuple-element.140), channel_id=1, source_target_pairs={{0,2},{1,3},{2,0},{3,1},{4,6},{5,7},{6,4},{7,5},{8,10},{9,11},{10,... | collective-permute-start | bytes 552968 | tf_op jit(solution)/shard_map/ppermute | solution.py:893
  302.3 6.8 %collective-permute-start.40 = (bf16[10,24,384]{2,1,0:T(8,128)(2,1)}, bf16[10,24,384]{2,1,0:T(8,128)(2,1)S(1)}, u32[]{:S(2)}, u32[]{:S(2)}) collective-permute-start(bf16[10,24,384]{2,1,0:T(8,128)(2,1)} %get-tuple-element.141), channel_id=1, source_target_pairs={{0,3},{1,0},{2,1},{3,2},{4,7},{5,4},{6,5},{7,6},{8,11},{9,8},{10,9... | collective-permute-start | bytes 552968 | tf_op jit(solution)/shard_map/ppermute | solution.py:893
  312.2 17.3 %collective-permute-start.47 = (f32[10,24,384]{2,1,0:T(8,128)}, f32[10,24,384]{2,1,0:T(8,128)S(1)}, u32[]{:S(2)}, u32[]{:S(2)}) collective-permute-start(f32[10,24,384]{2,1,0:T(8,128)} %get-tuple-element.153), channel_id=1, source_target_pairs={{0,4},{4,0},{8,12},{12,8},{16,20},{20,16},{24,28},{28,24},{1,5},{5... | collective-permute-start | bytes 1105928 | tf_op jit(solution)/shard_map/ppermute | solution.py:887
  316.0 6.9 %collective-permute-start.51 = (bf16[96,768]{1,0:T(8,128)(2,1)}, bf16[96,768]{1,0:T(8,128)(2,1)S(1)}, u32[]{:S(2)}, u32[]{:S(2)}) collective-permute-start(bf16[96,768]{1,0:T(8,128)(2,1)} %get-tuple-element.166), channel_id=1, source_target_pairs={{0,8},{4,12},{8,0},{12,4},{16,24},{20,28},{24,16},{28,20},{1,9},{5... | collective-permute-start | bytes 442376 | tf_op jit(solution)/shard_map/ppermute | solution.py:890
  317.5 9.3 %collective-permute-start.52 = (bf16[96,768]{1,0:T(8,128)(2,1)}, bf16[96,768]{1,0:T(8,128)(2,1)S(1)}, u32[]{:S(2)}, u32[]{:S(2)}) collective-permute-start(bf16[96,768]{1,0:T(8,128)(2,1)} %get-tuple-element.167), channel_id=1, source_target_pairs={{0,16},{4,20},{8,24},{12,28},{16,0},{20,4},{24,8},{28,12},{1,17},{... | collective-permute-start | bytes 442376 | tf_op jit(solution)/shard_map/ppermute | solution.py:890
  317.9 9.0 %collective-permute-start.53 = (bf16[96,768]{1,0:T(8,128)(2,1)}, bf16[96,768]{1,0:T(8,128)(2,1)S(1)}, u32[]{:S(2)}, u32[]{:S(2)}) collective-permute-start(bf16[96,768]{1,0:T(8,128)(2,1)} %get-tuple-element.168), channel_id=1, source_target_pairs={{0,24},{4,28},{8,16},{12,20},{16,8},{20,12},{24,0},{28,4},{1,25},{... | collective-permute-start | bytes 442376 | tf_op jit(solution)/shard_map/ppermute | solution.py:890
  336.8 12.3 %collective-permute-start.32 = (bf16[256,768]{1,0:T(8,128)(2,1)}, bf16[256,768]{1,0:T(8,128)(2,1)S(1)}, u32[]{:S(2)}, u32[]{:S(2)}) collective-permute-start(bf16[256,768]{1,0:T(8,128)(2,1)} %get-tuple-element.127), channel_id=1, source_target_pairs={{0,8},{4,12},{8,0},{12,4},{16,24},{20,28},{24,16},{28,20},{1,9},{5... | collective-permute-start | bytes 1179656 | tf_op jit(solution)/shard_map/ppermute | solution.py:890
  337.4 18.6 %collective-permute-start.33 = (bf16[256,768]{1,0:T(8,128)(2,1)}, bf16[256,768]{1,0:T(8,128)(2,1)S(1)}, u32[]{:S(2)}, u32[]{:S(2)}) collective-permute-start(bf16[256,768]{1,0:T(8,128)(2,1)} %get-tuple-element.128), channel_id=1, source_target_pairs={{0,16},{4,20},{8,24},{12,28},{16,0},{20,4},{24,8},{28,12},{1,17},{... | collective-permute-start | bytes 1179656 | tf_op jit(solution)/shard_map/ppermute | solution.py:890
  338.9 17.1 %collective-permute-start.34 = (bf16[256,768]{1,0:T(8,128)(2,1)}, bf16[256,768]{1,0:T(8,128)(2,1)S(1)}, u32[]{:S(2)}, u32[]{:S(2)}) collective-permute-start(bf16[256,768]{1,0:T(8,128)(2,1)} %get-tuple-element.129), channel_id=1, source_target_pairs={{0,24},{4,28},{8,16},{12,20},{16,8},{20,12},{24,0},{28,4},{1,25},{... | collective-permute-start | bytes 1179656 | tf_op jit(solution)/shard_map/ppermute | solution.py:890
  (52 other events, 698.0 us)
